TPU v7x, 128 devices: a whole 4x4x4 slice. The times are simulated.
128 devices in a mesh: dp: 4 (over z_lo, core), fsdp: 32 (over z_hi, y, x).
Axes of the slice: x: 4, y: 4, z: 4 (z_hi: 2, z_lo: 2; z = z_hi * 2 + z_lo), core: 2. Of those that a mesh axis runs over, the one named last changes fastest.
Arguments:
- tokens: bfloat16 [32768, 640], P(('dp', 'fsdp')), may hold values from -6 to 6
- cotangent: bfloat16 [3, 32768, 640], P(None, ('dp', 'fsdp')), may hold values from -6 to 6
- segment_ids: int32 [16, 2048], P('dp'), may hold values from 0 to 2, as said below
- width_mask: int32 [16, 3], P('dp'), may hold values from 0 to 1, as said below
- q_codes: bfloat16 [640, 1024], P(('dp', 'fsdp')), may hold values from -128 to 127, as said below
- kv_codes: bfloat16 [640, 512], P(('dp', 'fsdp')), may hold values from -128 to 127, as said below
- o_codes: bfloat16 [1024, 640], P(('dp', 'fsdp')), may hold values from -128 to 127, as said below
- gate_codes: bfloat16 [640, 2048], P(('dp', 'fsdp')), may hold values from -128 to 127, as said below
- up_codes: bfloat16 [640, 2048], P(('dp', 'fsdp')), may hold values from -128 to 127, as said below
- down_codes: bfloat16 [2048, 640], P(('dp', 'fsdp')), may hold values from -128 to 127, as said below
- q_scale: float32 [1024], P(('dp', 'fsdp')), may hold values from 1 to 4
- kv_scale: float32 [512], P(('dp', 'fsdp')), may hold values from 1 to 4
- o_scale: float32 [640], P(('dp', 'fsdp')), may hold values from 1 to 4
- gate_scale: float32 [2048], P(('dp', 'fsdp')), may hold values from 1 to 4
- up_scale: float32 [2048], P(('dp', 'fsdp')), may hold values from 1 to 4
- down_scale: float32 [640], P(('dp', 'fsdp')), may hold values from 1 to 4
- norm_gains: float32 [640, 4], P(('dp', 'fsdp')), may hold values from 0.5 to 1.5
Outputs:
- outputs: float32 [3, 32768, 640], P(None, ('dp', 'fsdp'))
- grad_tokens: float32 [32768, 640], P(('dp', 'fsdp'))
- grad_q_codes: float32 [640, 1024], P(('dp', 'fsdp'))
- grad_kv_codes: float32 [640, 512], P(('dp', 'fsdp'))
- grad_o_codes: float32 [1024, 640], P(('dp', 'fsdp'))
- grad_gate_codes: float32 [640, 2048], P(('dp', 'fsdp'))
- grad_up_codes: float32 [640, 2048], P(('dp', 'fsdp'))
- grad_down_codes: float32 [2048, 640], P(('dp', 'fsdp'))
- grad_q_scale: float32 [1024], P(('dp', 'fsdp'))
- grad_kv_scale: float32 [512], P(('dp', 'fsdp'))
- grad_o_scale: float32 [640], P(('dp', 'fsdp'))
- grad_gate_scale: float32 [2048], P(('dp', 'fsdp'))
- grad_up_scale: float32 [2048], P(('dp', 'fsdp'))
- grad_down_scale: float32 [640], P(('dp', 'fsdp'))
- grad_norm_gains: float32 [640, 4], P(('dp', 'fsdp'))
Inputs may be any that keep to these rules, and one draw needn't show every extreme that they name: `width_mask`: every sequence runs at least one width. `q_codes`: whole numbers. `kv_codes`: whole numbers. `o_codes`: whole numbers. `gate_codes`: whole numbers. `up_codes`: whole numbers. `down_codes`: whole numbers. `segment_ids`: each sequence's ids start at 0 and never fall.
All inputs are finite; a program needn't handle non-finite values.
Results may differ from a plain program's by a relative error of at most 0.024.
Values may be sent and summed in bfloat16 or wider, within the bound.
No kernel may reach another device: no remote copies, remote signals or barrier semaphores. Data moves between devices by JAX's collectives and lax.ppermute only.
A program may use at most 320 MiB of HBM per device.

v0:
```python
import math

import jax
import jax.numpy as jnp
from jax import lax
from jax.sharding import PartitionSpec as P

WINDOW = 512


epsilon = 1e-06
soft_cap = 50.0
masked_value = -1e30


def joined_along(pieces, dim):
    lengths = list(pieces.shape[1:])
    lengths[dim] *= pieces.shape[0]
    return jnp.moveaxis(pieces, 0, dim).reshape(lengths)


def gather_packed(arrays, axis, dims):
    ravelled = jnp.concatenate([a.reshape(-1) for a in arrays])
    lines, at, done = (lax.all_gather(ravelled, axis), 0, [])
    for a, dim in zip(arrays, dims):
        pieces = lines[:, at : at + a.size].reshape(-1, *a.shape)
        done.append(joined_along(pieces, dim))
        at += a.size
    return tuple(done)


def side_by_side(arrays, axis, dim, along):
    columns = [a.reshape(*a.shape[:along], -1) for a in arrays]
    both = jnp.concatenate(columns, axis=along)
    out, at, done = (lax.all_gather(both, axis, axis=dim, tiled=True), 0, [])
    for a, column in zip(arrays, columns):
        share = out[..., at : at + column.shape[along]]
        done.append(share.reshape(*share.shape[:along], *a.shape[along:]))
        at += column.shape[along]
    return tuple(done)


def from_behind(value, axis, steps):
    count = lax.axis_size(axis)
    leading, last = (max(0, -steps), min(count, count - steps))
    return lax.ppermute(value, axis, [(source, source + steps) for source in range(leading, last)])


def split_up(shard, dim, peers):
    lengths = shard.shape
    pieces = shard.reshape(*lengths[:dim], peers, lengths[dim] // peers, *lengths[dim + 1 :])
    return jnp.moveaxis(pieces, dim, 0)


def one_scatter(arrays, axis, dims):
    peers = lax.axis_size(axis)
    pieces = [split_up(a, dim, peers) for a, dim in zip(arrays, dims)]
    lines = jnp.concatenate([b.reshape(peers, -1) for b in pieces], axis=1)
    span = max(16, -(-lines.shape[1] // 1024) * 8)
    lines = jnp.pad(lines, ((0, 0), (0, span * 128 - lines.shape[1]))).reshape(-1, 128)
    ravelled, at, done = (lax.psum_scatter(lines, axis, tiled=True).reshape(-1), 0, [])
    for b in pieces:
        part = b[0]
        done.append(ravelled[at : at + part.size].reshape(part.shape))
        at += part.size
    return tuple(done)


def norm_rows(values, gain_row):
    return (
        values * lax.rsqrt(jnp.mean(values * values, axis=-1, keepdims=True) + epsilon) * gain_row
    )


def norm_back(values, gain_row, grad_rows):
    unused, pullback = jax.vjp(norm_rows, values, gain_row)
    return pullback(grad_rows)


def rotate(values, cosine, sine_table):
    half_size = values.shape[-1] // 2
    first_half = values[..., :half_size]
    second_half = values[..., half_size:]
    return jnp.concatenate(
        [
            first_half * cosine - second_half * sine_table,
            second_half * cosine + first_half * sine_table,
        ],
        axis=-1,
    )


def unrotate(values, cosine, sine_table):
    half_size = values.shape[-1] // 2
    first_half = values[..., :half_size]
    second_half = values[..., half_size:]
    return jnp.concatenate(
        [
            first_half * cosine + second_half * sine_table,
            second_half * cosine - first_half * sine_table,
        ],
        axis=-1,
    )


def rotary_tables(position, head_size):
    inverse = 10000.0 ** (-2.0 * jnp.arange(head_size // 2).astype(jnp.float32) / head_size)
    angles = position[:, None] * inverse[None, :]
    return (jnp.cos(angles), jnp.sin(angles))


def sliced(code_table, bit_count):
    step_size = 2.0 ** (8 - bit_count)
    return jnp.floor(code_table / step_size) * step_size + step_size / 2.0


def unit_scale(fan_in):
    return 1.0 / (128.0 * math.sqrt(fan_in))


def outer_sum(left, right):
    return lax.dot_general(
        left, right, (((0,), (0,)), ((), ())), preferred_element_type=jnp.float32
    )


def back_mul(grad_rows, matrix):
    return lax.dot_general(
        grad_rows,
        matrix,
        (((grad_rows.ndim - 1,), (1,)), ((), ())),
        preferred_element_type=jnp.float32,
    )


def dequant(code_list, scale_list, bit_count):
    return [
        (
            scale_row[None, :]
            * sliced(code_table.astype(jnp.float32), bit_count)
            * unit_scale(code_table.shape[0])
        ).astype(jnp.bfloat16)
        for code_table, scale_row in zip(code_list, scale_list)
    ]


def capped_scores(queries, key_rows, allowed):
    head_size = queries.shape[-1]
    scores = jnp.einsum(
        "qhd,kd->hqk", queries, key_rows, preferred_element_type=jnp.float32
    ) * head_size ** (-0.5)
    tangent = jnp.tanh(scores / soft_cap)
    return (jnp.where(allowed, soft_cap * tangent, masked_value), tangent)


def project_width(operands):
    normed, w_query, w_keyval, cosine, sine_table = operands
    tok_dev = normed.shape[0]
    head_size = cosine.shape[-1] * 2
    head_count = w_query.shape[1] // head_size
    queries = jnp.dot(normed, w_query, preferred_element_type=jnp.float32).reshape(
        tok_dev, head_count, head_size
    )
    queries = rotate(queries, cosine[:, None, :], sine_table[:, None, :]).astype(jnp.bfloat16)
    keyval = jnp.dot(normed, w_keyval, preferred_element_type=jnp.float32)
    key_value = jnp.concatenate(
        [rotate(keyval[:, :head_size], cosine, sine_table), keyval[:, head_size:]], axis=-1
    ).astype(jnp.bfloat16)
    return (queries, key_value)


def attend_width(operands):
    tokens_f, queries, key_value, allowed, matrices, gain_table = operands
    w_out, w_gate, w_up, w_down = (matrices[2], matrices[3], matrices[4], matrices[5])
    tok_dev, head_count, head_size = queries.shape
    key_rows = key_value[:, :head_size]
    value_rows = key_value[:, head_size:]
    capped, tangent = capped_scores(queries, key_rows, allowed)
    row_peak = jnp.max(capped, axis=-1, keepdims=True)
    log_total = row_peak + jnp.log(jnp.sum(jnp.exp(capped - row_peak), axis=-1, keepdims=True))
    weights_soft = jnp.exp(capped - log_total).astype(jnp.bfloat16)
    mixed = jnp.einsum("hqk,kd->qhd", weights_soft, value_rows, preferred_element_type=jnp.float32)
    mixed = mixed.astype(jnp.bfloat16).reshape(tok_dev, head_count * head_size)
    attended = jnp.dot(mixed, w_out, preferred_element_type=jnp.float32)
    middle = tokens_f + norm_rows(attended, gain_table[:, 1])
    normed_two = norm_rows(middle, gain_table[:, 2]).astype(jnp.bfloat16)
    gate_rows = jnp.dot(normed_two, w_gate, preferred_element_type=jnp.float32)
    up_rows = jnp.dot(normed_two, w_up, preferred_element_type=jnp.float32)
    hidden = (jax.nn.gelu(gate_rows, approximate=True) * up_rows).astype(jnp.bfloat16)
    branch = jnp.dot(hidden, w_down, preferred_element_type=jnp.float32)
    result = middle + norm_rows(branch, gain_table[:, 3])
    return (
        result,
        (
            queries,
            key_value,
            log_total,
            mixed,
            attended,
            middle,
            normed_two,
            gate_rows,
            up_rows,
            hidden,
            branch,
        ),
    )


def back_attend(operands):
    grad_result, allowed, matrices, gain_table, cosine, sine_table, stored = operands
    w_out, w_gate, w_up, w_down = (matrices[2], matrices[3], matrices[4], matrices[5])
    (
        queries,
        key_value,
        log_total,
        mixed,
        attended,
        middle,
        normed_two,
        gate_rows,
        up_rows,
        hidden,
        branch,
    ) = stored
    tok_dev, head_count, head_size = queries.shape
    key_rows = key_value[:, :head_size]
    value_rows = key_value[:, head_size:]
    grad_branch, gain_three = norm_back(branch, gain_table[:, 3], grad_result)
    grad_branch = grad_branch.astype(jnp.bfloat16)
    grad_down = outer_sum(hidden, grad_branch)
    grad_hidden = back_mul(grad_branch, w_down)
    unused, pullback = jax.vjp(
        lambda first_in, second_in: jax.nn.gelu(first_in, approximate=True) * second_in,
        gate_rows,
        up_rows,
    )
    grad_gate_rows, grad_up_rows = pullback(grad_hidden)
    grad_gate_rows = grad_gate_rows.astype(jnp.bfloat16)
    grad_up_rows = grad_up_rows.astype(jnp.bfloat16)
    grad_gate = outer_sum(normed_two, grad_gate_rows)
    grad_up = outer_sum(normed_two, grad_up_rows)
    grad_normed_two = back_mul(grad_gate_rows, w_gate) + back_mul(grad_up_rows, w_up)
    grad_inner, gain_two = norm_back(middle, gain_table[:, 2], grad_normed_two)
    grad_middle = grad_result + grad_inner
    grad_attended, gain_one = norm_back(attended, gain_table[:, 1], grad_middle)
    grad_attended = grad_attended.astype(jnp.bfloat16)
    grad_out = outer_sum(mixed, grad_attended)
    grad_mixed = (
        back_mul(grad_attended, w_out).astype(jnp.bfloat16).reshape(tok_dev, head_count, head_size)
    )
    capped, tangent = capped_scores(queries, key_rows, allowed)
    weights_soft = jnp.exp(capped - log_total)
    grad_soft = jnp.einsum(
        "qhd,kd->hqk", grad_mixed, value_rows, preferred_element_type=jnp.float32
    )
    grad_values = jnp.einsum(
        "hqk,qhd->kd",
        weights_soft.astype(jnp.bfloat16),
        grad_mixed,
        preferred_element_type=jnp.float32,
    )
    grad_capped = weights_soft * (
        grad_soft - jnp.sum(weights_soft * grad_soft, axis=-1, keepdims=True)
    )
    grad_scores = (grad_capped * (1.0 - tangent * tangent)).astype(jnp.bfloat16)
    grad_queries = jnp.einsum(
        "hqk,kd->qhd", grad_scores, key_rows, preferred_element_type=jnp.float32
    ) * head_size ** (-0.5)
    grad_keys = jnp.einsum(
        "hqk,qhd->kd", grad_scores, queries, preferred_element_type=jnp.float32
    ) * head_size ** (-0.5)
    grad_query_raw = (
        unrotate(grad_queries, cosine[:, None, :], sine_table[:, None, :])
        .astype(jnp.bfloat16)
        .reshape(tok_dev, head_count * head_size)
    )
    key_value_grads = jnp.concatenate([grad_keys, grad_values], axis=-1)
    return (
        grad_middle,
        grad_query_raw,
        key_value_grads,
        (grad_out, grad_gate, grad_up, grad_down),
        (gain_one, gain_two, gain_three),
    )


def finish_width(operands):
    normed, carried, grad_query_raw, w_query, w_keyval, cosine, sine_table = operands
    head_size = cosine.shape[-1] * 2
    grad_keyval = jnp.concatenate(
        [unrotate(carried[:, :head_size], cosine, sine_table), carried[:, head_size:]], axis=-1
    ).astype(jnp.bfloat16)
    grad_query = outer_sum(normed, grad_query_raw)
    grad_kv = outer_sum(normed, grad_keyval)
    grad_in = back_mul(grad_query_raw, w_query) + back_mul(grad_keyval, w_keyval)
    return (grad_query, grad_kv, grad_in)


def per_device(
    tokens,
    cotangent,
    segment_ids,
    width_mask,
    q_codes,
    kv_codes,
    o_codes,
    gate_codes,
    up_codes,
    down_codes,
    q_scale,
    kv_scale,
    o_scale,
    gate_scale,
    up_scale,
    down_scale,
    norm_gains,
):
    code_list = list(
        gather_packed(
            (q_codes, kv_codes, o_codes, gate_codes, up_codes, down_codes),
            ("dp", "fsdp"),
            (0, 0, 0, 0, 0, 0),
        )
    )
    small_params = (
        lax.all_gather(q_scale, ("dp", "fsdp"), axis=0, tiled=True),
        lax.all_gather(kv_scale, ("dp", "fsdp"), axis=0, tiled=True),
        lax.all_gather(o_scale, ("dp", "fsdp"), axis=0, tiled=True),
        lax.all_gather(gate_scale, ("dp", "fsdp"), axis=0, tiled=True),
        lax.all_gather(up_scale, ("dp", "fsdp"), axis=0, tiled=True),
        *side_by_side((down_scale, norm_gains), ("dp", "fsdp"), 0, 1),
    )
    scale_list = list(small_params[:6])
    gain_table = small_params[6]
    tokens_f = tokens.astype(jnp.float32)
    tok_dev, model_width = tokens.shape
    head_size = kv_codes.shape[1] // 2
    reach_count = (WINDOW + tok_dev - 2) // tok_dev
    split_count = segment_ids.shape[1] // tok_dev
    device_place = lax.axis_index("fsdp")
    seq_slot = device_place // split_count
    offset = device_place % split_count * tok_dev
    my_segments = lax.dynamic_slice_in_dim(segment_ids, seq_slot, 1, 0)[0]
    my_widths = lax.dynamic_slice_in_dim(width_mask, seq_slot, 1, 0)[0]
    key_count = (reach_count + 1) * tok_dev
    query_pos = offset + jnp.arange(tok_dev, dtype=jnp.int32)
    key_pos = offset - reach_count * tok_dev + jnp.arange(key_count, dtype=jnp.int32)
    padded_segments = jnp.concatenate(
        [jnp.full((reach_count * tok_dev,), -1, jnp.int32), my_segments]
    )
    key_segments = lax.dynamic_slice_in_dim(padded_segments, offset, key_count)
    query_segments = lax.dynamic_slice_in_dim(my_segments, offset, tok_dev)
    distance = query_pos[:, None] - key_pos[None, :]
    allowed = (
        (key_pos[None, :] >= 0)
        & (distance >= 0)
        & (distance < WINDOW)
        & (query_segments[:, None] == key_segments[None, :])
    )[None]
    cosine, sine_table = rotary_tables(query_pos.astype(jnp.float32), head_size)
    normed = norm_rows(tokens_f, gain_table[:, 0]).astype(jnp.bfloat16)
    bit_list = (8, 4, 2)
    matrices_all = [dequant(code_list, scale_list, bit_count) for bit_count in bit_list]
    query_list = []
    local_list = []
    for width_index in range(3):
        matrices = matrices_all[width_index]
        queries, key_value = project_width((normed, matrices[0], matrices[1], cosine, sine_table))
        query_list.append(queries)
        local_list.append(key_value)
    local_stack = jnp.stack(local_list)
    pieces = [local_stack]
    moving = local_stack
    for block_index in range(reach_count):
        moving = from_behind(moving, "fsdp", 1)
        pieces.insert(0, moving)
    window_stack = jnp.concatenate(pieces, axis=1)
    results = []
    stored_all = []
    for width_index in range(3):
        result, stored = attend_width(
            (
                tokens_f,
                query_list[width_index],
                window_stack[width_index],
                allowed,
                matrices_all[width_index],
                gain_table,
            )
        )
        keep_rows = my_widths[width_index] > 0
        results.append(jnp.where(keep_rows, result, 0.0))
        stored_all.append(stored)
    outputs = jnp.stack(results)
    grad_rest = jnp.zeros_like(tokens_f)
    grad_normed = jnp.zeros_like(tokens_f)
    code_grads = [jnp.zeros(code_table.shape, jnp.float32) for code_table in code_list]
    scale_grads = [jnp.zeros(scale_row.shape, jnp.float32) for scale_row in scale_list]
    gain_sums = [jnp.zeros((model_width,), jnp.float32) for gain_index in range(3)]
    back_matrices = []
    query_grads = []
    window_grads = []
    late_grads = []
    for width_index in range(3):
        matrices = matrices_all[width_index]
        back_matrices.append(matrices)
        keep_rows = my_widths[width_index] > 0
        grad_result = jnp.where(keep_rows, cotangent[width_index].astype(jnp.float32), 0.0)
        grad_middle, grad_query_raw, key_value_grads, matrix_late, gain_parts = back_attend(
            (
                grad_result,
                allowed,
                matrices,
                gain_table,
                cosine,
                sine_table,
                stored_all[width_index],
            )
        )
        grad_rest = grad_rest + grad_middle
        query_grads.append(grad_query_raw)
        window_grads.append(key_value_grads)
        late_grads.append(matrix_late)
        for gain_index in range(3):
            gain_sums[gain_index] = gain_sums[gain_index] + gain_parts[gain_index]
    grad_stack = jnp.stack(window_grads)
    carried = grad_stack[:, 0:tok_dev]
    for block_index in range(1, reach_count + 1):
        carried = (
            from_behind(carried, "fsdp", -1)
            + grad_stack[:, block_index * tok_dev : (block_index + 1) * tok_dev]
        )
    for width_index in range(3):
        bit_count = bit_list[width_index]
        matrices = back_matrices[width_index]
        grad_query, grad_kv, grad_in = finish_width(
            (
                normed,
                carried[width_index],
                query_grads[width_index],
                matrices[0],
                matrices[1],
                cosine,
                sine_table,
            )
        )
        grad_normed = grad_normed + grad_in
        matrix_grads = (grad_query, grad_kv) + tuple(late_grads[width_index])
        levels = [sliced(code_table.astype(jnp.float32), bit_count) for code_table in code_list]
        for matrix_index in range(6):
            scaled = matrix_grads[matrix_index] * unit_scale(code_list[matrix_index].shape[0])
            code_grads[matrix_index] = (
                code_grads[matrix_index] + scaled * scale_list[matrix_index][None, :]
            )
            scale_grads[matrix_index] = scale_grads[matrix_index] + jnp.sum(
                scaled * levels[matrix_index], axis=0
            )
    grad_first, gain_first = norm_back(tokens_f, gain_table[:, 0], grad_normed)
    grad_tokens = grad_rest + grad_first
    gain_total = jnp.stack([gain_first, gain_sums[0], gain_sums[1], gain_sums[2]], axis=1)
    shares = one_scatter(
        (
            code_grads[0],
            code_grads[1],
            code_grads[2],
            code_grads[3],
            code_grads[4],
            code_grads[5],
            scale_grads[0],
            scale_grads[1],
            scale_grads[2],
            scale_grads[3],
            scale_grads[4],
            scale_grads[5],
            gain_total,
        ),
        ("dp", "fsdp"),
        (0, 0, 0, 0, 0, 0, 0, 0, 0, 0, 0, 0, 0),
    )
    return (
        outputs,
        grad_tokens,
        shares[0],
        shares[1],
        shares[2],
        shares[3],
        shares[4],
        shares[5],
        shares[6],
        shares[7],
        shares[8],
        shares[9],
        shares[10],
        shares[11],
        shares[12],
    )


def solution(mesh):
    return jax.shard_map(
        per_device,
        mesh=mesh,
        in_specs=(
            P(("dp", "fsdp"), None),
            P(None, ("dp", "fsdp"), None),
            P("dp", None),
            P("dp", None),
            P(("dp", "fsdp"), None),
            P(("dp", "fsdp"), None),
            P(("dp", "fsdp"), None),
            P(("dp", "fsdp"), None),
            P(("dp", "fsdp"), None),
            P(("dp", "fsdp"), None),
            P(("dp", "fsdp")),
            P(("dp", "fsdp")),
            P(("dp", "fsdp")),
            P(("dp", "fsdp")),
            P(("dp", "fsdp")),
            P(("dp", "fsdp")),
            P(("dp", "fsdp"), None),
        ),
        out_specs=(
            P(None, ("dp", "fsdp"), None),
            P(("dp", "fsdp"), None),
            P(("dp", "fsdp"), None),
            P(("dp", "fsdp"), None),
            P(("dp", "fsdp"), None),
            P(("dp", "fsdp"), None),
            P(("dp", "fsdp"), None),
            P(("dp", "fsdp"), None),
            P(("dp", "fsdp")),
            P(("dp", "fsdp")),
            P(("dp", "fsdp")),
            P(("dp", "fsdp")),
            P(("dp", "fsdp")),
            P(("dp", "fsdp")),
            P(("dp", "fsdp"), None),
        ),
        check_vma=False,
    )
```

profile of v0, /device:TPU:8, one launch (start us, length us, event | category | flops | bytes accessed | tf_op | source)
XLA Modules:
  0.0 1239.3 jit_solution(14979858596259422661)
XLA Ops:
  23.0 67.2 %all-reduce.8 = (f32[512]{0:T(512)S(1)}, f32[1024]{0:T(1024)S(1)}, f32[640]{0:T(1024)S(1)}, f32[2048]{0:T(1024)S(1)}, f32[2048]{0:T(1024)S(1)}) all-reduce(f32[512]{0:T(512)S(1)} %dynamic-update-slice, f32[1024]{0:T(1024)S(1)} %dynamic-update-slice.1, f32[640]{0:T(1024)S(1)} %dynamic-update-slice.2, ...), channel_id=1, replica_groups=mesh['dp'=4,'fsdp'=32] {'dp','fsdp'}, use_global_device_ids=true, to_apply=%add.2 | all-reduce | flops 6272 | bytes 50176
  91.5 322.5 %all-gather.1 = f32[128,5,5]{2,1,0:T(8,128)S(1)} all-gather(f32[1,5,5]{2,1,0:T(8,128)S(1)} %maximum_bitcast_fusion.3), channel_id=1, replica_groups=mesh['dp'=4,'fsdp'=32] {'dp','fsdp'}, dimensions={0}, use_global_device_ids=true | all-gather | bytes 12900 | tf_op jit(solution)/shard_map/all_gather | solution.py:35
  423.2 10.5 copy.260
  436.3 17.1 %fusion.17 = (f32[128,10240]{1,0:T(8,128)}, f32[128,10240]{1,0:T(8,128)}, f32[128,10240]{1,0:T(8,128)}, f32[128,10240]{1,0:T(8,128)}, f32[128,10240]{1,0:T(8,128...) fusion(bf16[128,43520]{1,0:T(8,128)(2,1)S(1)} %bitcast.550), kind=kLoop, calls=%fused_computation.27 | loop fusion | flops 43253760 | bytes 55050240 | tf_op jit(solution)/shard_map/add | solution.py:114
  467.4 5.6 collective-permute-start
  473.0 10.2 multiply_convert_fusion.13
  517.1 6.0 fusion.160
  530.4 5.6 add.628
  536.0 5.8 reshape.908
  541.8 5.9 reshape.900
  547.7 5.8 reshape.910
  553.5 5.9 reshape.902
  559.3 5.5 reshape.912
  570.3 5.8 add.626
  576.2 5.8 add.622
  584.1 6.0 collective-permute-start.1
  593.6 6.7 collective-permute-done.1
  634.1 6.3 multiply_convert_fusion.26
  686.9 8.7 fusion.151
  695.6 8.9 fusion.177
  716.2 8.4 fusion.178
  724.6 8.6 fusion.149
  746.6 8.9 fusion.179
  755.5 8.7 fusion.147
  802.3 12.4 %multiply_reduce_fusion.4 = (f32[2048]{0:T(1024)S(1)}, f32[640,2048]{1,0:T(8,128)}, f32[2048]{0:T(1024)S(1)}, f32[2048]{0:T(1024)S(1)}) fusion(f32[640,2048]{1,0:T(8,128)} %reshape.902, f32[2048]{0:T(1024)S(1)} %copy-done.158, f32[640,2048]{1,0:T(8,128)} %fusion.427, f32[640,2048]{1,0:T(8,128)} %fusion.426, f32[640,2048]{1,0:T(8,128)} %add.626, ...), kind=kOutput, calls=%fused_computation.41 | convolution fusion | flops 686811136 | bytes 32866304 | tf_op jit(solution)/shard_map/dot_general | solution.py:122
  817.4 6.9 multiply_reduce_fusion.7
  827.2 8.3 multiply_reduce_fusion.1
  860.1 6.3 reshape_reshape.30
  866.4 6.5 reshape_reshape.31
  928.3 16.3 %pad.5 = f32[128,44032]{1,0:T(8,128)} pad(f32[128,43594]{1,0:T(8,128)} %dynamic-update-slice.17, f32[]{:T(128)} %constant.154.clone.1), padding=0_0x0_438 | pad | bytes 44864516 | tf_op jit(solution)/shard_map/jit(_pad)/pad | solution.py:60
  944.6 21.5 %reshape.884 = f32[44032,128]{1,0:T(8,128)} reshape(f32[128,44032]{1,0:T(8,128)} %pad.5) | data formatting | bytes 45088768 | tf_op jit(solution)/shard_map/reshape | solution.py:60
  971.8 250.3 %all-reduce.11.cloned.1.call-done = f32[44032,128]{1,0:T(8,128)} async-done(((f32[44032,128]{1,0:T(8,128)}), f32[44032,128]{1,0:T(8,128)}) %all-reduce.11.cloned.1.call-update) | async-done | bytes 22544400
  (704 shorter events, 335.1 us)
Async XLA Ops:
  7.2 416.0 %all-gather.5.cloned.1.call-start = ((), (), s32[]{:S(2)}) async-start(), calls=%async_computation | async-start | bytes 22456320 | tf_op jit(solution)/shard_map/all_gather | solution.py:24
  14.7 1207.4 %all-reduce.11.cloned.1.call-start = ((), (), s32[]{:S(2)}) async-start(), calls=%async_computation.1 | async-start | bytes 45088768
  90.2 343.5 %copy-start.145 = (f32[2048]{0:T(1024)}, f32[2048]{0:T(1024)S(1)}, u32[]{:S(2)}) copy-start(f32[2048]{0:T(1024)S(1)} %get-tuple-element.112) | copy-start | bytes 24580
  90.2 343.5 %copy-start.149 = (f32[640]{0:T(1024)}, f32[640]{0:T(1024)S(1)}, u32[]{:S(2)}) copy-start(f32[640]{0:T(1024)S(1)} %get-tuple-element.111) | copy-start | bytes 7684
  90.2 343.5 %copy-start.155 = (f32[1024]{0:T(1024)}, f32[1024]{0:T(1024)S(1)}, u32[]{:S(2)}) copy-start(f32[1024]{0:T(1024)S(1)} %get-tuple-element.110) | copy-start | bytes 12292
  90.2 371.1 %copy-start.152 = (f32[512]{0:T(512)}, f32[512]{0:T(512)S(1)}, u32[]{:S(2)}) copy-start(f32[512]{0:T(512)S(1)} %get-tuple-element.109) | copy-start | bytes 6148
  414.9 48.6 %copy-start.180 = (f32[128]{0:T(128)}, f32[128]{0:T(128)S(1)}, u32[]{:S(2)}) copy-start(f32[128]{0:T(128)S(1)} %multiply_power_fusion) | copy-start | bytes 1540
  414.9 48.5 %copy-start.173 = (f32[256]{0:T(256)}, f32[256]{0:T(256)S(1)}, u32[]{:S(2)}) copy-start(f32[256]{0:T(256)S(1)} %fusion.310) | copy-start | bytes 3076
  416.9 16.8 %copy-start.171 = (f32[256]{0:T(256)}, f32[256]{0:T(256)S(1)}, u32[]{:S(2)}) copy-start(f32[256]{0:T(256)S(1)} %fusion.214) | copy-start | bytes 3076
  418.3 15.5 %copy-start.147 = (f32[640]{0:T(1024)}, f32[640]{0:T(1024)S(1)}, u32[]{:S(2)}) copy-start(f32[640]{0:T(1024)S(1)} %get-tuple-element.100) | copy-start | bytes 7684
  433.8 19.6 %copy-start.3 = (bf16[128,1,43520]{2,0,1:T(8,128)(2,1)}, bf16[128,1,43520]{2,0,1:T(8,128)(2,1)S(1)}, u32[]{:S(2)}) copy-start(bf16[128,1,43520]{2,0,1:T(8,128)(2,1)S(1)} %copy.260) | copy-start | bytes 33423364
  461.3 21.9 %copy-start.14 = (f32[640,512]{1,0:T(8,128)}, f32[640,512]{1,0:T(8,128)S(1)}, u32[]{:S(2)}) copy-start(f32[640,512]{1,0:T(8,128)S(1)} %reshape.894) | copy-start | bytes 3932164
  467.4 116.7 %collective-permute-start = (bf16[3,256,512]{2,1,0:T(8,128)(2,1)}, bf16[3,256,512]{2,1,0:T(8,128)(2,1)}, u32[]{:S(2)}, u32[]{:S(2)}) collective-permute-start(bf16[3,256,512]{2,1,0:T(8,128)(2,1)} %maximum_maximum_fusion.1), channel_id=1, source_target_pairs={{0,1},{1,2},{2,3},{3,4},{4,5},{5,6},{6,7},{7,8},{8,9},{9,10},{10,1... | collective-permute-start | bytes 2359304 | tf_op jit(solution)/shard_map/ppermute | solution.py:46
  584.1 16.2 %collective-permute-start.1 = (bf16[3,256,512]{2,1,0:T(8,128)(2,1)}, bf16[3,256,512]{2,1,0:T(8,128)(2,1)S(1)}, u32[]{:S(2)}, u32[]{:S(2)}) collective-permute-start(bf16[3,256,512]{2,1,0:T(8,128)(2,1)} %collective-permute-done), channel_id=1, source_target_pairs={{0,1},{1,2},{2,3},{3,4},{4,5},{5,6},{6,7},{7,8},{8,9},{9,10},{10,1... | collective-permute-start | bytes 2359304 | tf_op jit(solution)/shard_map/ppermute | solution.py:46
  593.6 10.9 copy-start.137
  593.6 10.9 copy-start.138
  593.6 12.3 copy-start.135
  593.6 12.3 copy-start.136
  625.8 15.8 %copy-start.41 = (f32[256,640]{1,0:T(8,128)}, f32[256,640]{1,0:T(8,128)S(1)}, u32[]{:S(2)}) copy-start(f32[256,640]{1,0:T(8,128)S(1)} %get-tuple-element.283) | copy-start | bytes 1966084
  785.7 49.8 %collective-permute-start.2 = (f32[3,256,512]{2,1,0:T(8,128)}, f32[3,256,512]{2,1,0:T(8,128)}, u32[]{:S(2)}, u32[]{:S(2)}) collective-permute-start(f32[3,256,512]{2,1,0:T(8,128)} %slice.400), channel_id=1, source_target_pairs={{1,0},{2,1},{3,2},{4,3},{5,4},{6,5},{7,6},{8,7},{9,8},{10,9},{11,1... | collective-permute-start | bytes 4718600 | tf_op jit(solution)/shard_map/ppermute | solution.py:46
  802.2 12.5 %slice-start.2 = ((s8[5242880]{0:T(1024)(128)(4,1)}), s8[4194304]{0:T(1024)(128)(4,1)S(1)}, s32[]{:S(2)}) async-start(s8[5242880]{0:T(1024)(128)(4,1)} %bitcast.521), calls=%async_computation.4 | async-start | bytes 8388608
  802.2 12.5 %slice-start.6 = ((s8[5242880]{0:T(1024)(128)(4,1)}), s8[4194304]{0:T(1024)(128)(4,1)S(1)}, s32[]{:S(2)}) async-start(s8[5242880]{0:T(1024)(128)(4,1)} %bitcast.525), calls=%async_computation.8 | async-start | bytes 8388608
  802.2 14.1 %slice-start.10 = ((s8[5242880]{0:T(1024)(128)(4,1)}), s8[4194304]{0:T(1024)(128)(4,1)S(1)}, s32[]{:S(2)}) async-start(s8[5242880]{0:T(1024)(128)(4,1)} %bitcast.529), calls=%async_computation.12 | async-start | bytes 8388608
  802.2 14.3 %slice-start.3 = ((s8[5242880]{0:T(1024)(128)(4,1)}), s8[1048576]{0:T(1024)(128)(4,1)S(1)}, s32[]{:S(2)}) async-start(s8[5242880]{0:T(1024)(128)(4,1)} %bitcast.521), calls=%async_computation.5 | async-start | bytes 2097152
  802.2 14.5 %slice-start.7 = ((s8[5242880]{0:T(1024)(128)(4,1)}), s8[1048576]{0:T(1024)(128)(4,1)S(1)}, s32[]{:S(2)}) async-start(s8[5242880]{0:T(1024)(128)(4,1)} %bitcast.525), calls=%async_computation.9 | async-start | bytes 2097152
  802.3 14.8 %slice-start.11 = ((s8[5242880]{0:T(1024)(128)(4,1)}), s8[1048576]{0:T(1024)(128)(4,1)S(1)}, s32[]{:S(2)}) async-start(s8[5242880]{0:T(1024)(128)(4,1)} %bitcast.529), calls=%async_computation.13 | async-start | bytes 2097152
  802.3 15.1 %copy-start.68 = (bf16[256,2048]{1,0:T(8,128)(2,1)S(1)}, bf16[256,2048]{1,0:T(8,128)(2,1)}, u32[]{:S(2)}) copy-start(bf16[256,2048]{1,0:T(8,128)(2,1)} %get-tuple-element.168) | copy-start | bytes 3145732
  802.3 15.1 %copy-start.157 = (f32[2048]{0:T(1024)S(1)}, f32[2048]{0:T(1024)}, u32[]{:S(2)}) copy-start(f32[2048]{0:T(1024)} %get-tuple-element.294) | copy-start | bytes 24580
  838.8 11.9 copy-start.22
  838.8 39.9 %collective-permute-start.3 = (f32[3,256,512]{2,1,0:T(8,128)}, f32[3,256,512]{2,1,0:T(8,128)}, u32[]{:S(2)}, u32[]{:S(2)}) collective-permute-start(f32[3,256,512]{2,1,0:T(8,128)} %slice_add_fusion.1), channel_id=1, source_target_pairs={{1,0},{2,1},{3,2},{4,3},{5,4},{6,5},{7,6},{8,7},{9,8},{10,9},{11,1... | collective-permute-start | bytes 4718600 | tf_op jit(solution)/shard_map/ppermute | solution.py:46
  914.3 12.4 copy-start.144
  967.2 265.0 %copy-start.1 = (s32[4,3]{1,0:T(4,128)S(1)}, s32[4,3]{1,0:T(4,128)}, u32[]{:S(2)}) copy-start(s32[4,3]{1,0:T(4,128)} %param.20) | copy-start | bytes 148
  (190 other events, 760.9 us)
Sparse Core Ops, SparseCore 0:
  14.8 337.2 all-gather.4
  966.2 255.7 all-reduce.10
where the time goes:
time: 1250 us; the launch traced here: 1240 us
  blocking collectives  390 us (31%)
  local copies, waits for them, and re-layouts  266 us (21%)
  waiting for transfers between devices  257 us (21%)
  matrix products  215 us (17%)
  other arithmetic  72.9 us (6%)
  starting transfers between devices  20.1 us (2%)
  between operations  19.1 us (2%)
    all_gather x1, blocking collectives, side_by_side(): out, at, done = (lax.all_gather(both, axis, axis=dim, tiled=True), 0, [])  323 us
    unnamed x3, waiting for transfers between devices  250 us
    add x18, local copies, waits for them, and re-layouts, sliced(): return jnp.floor(code_table / step_size) * step_size + step_size / 2.0  74.4 us
    dot_general x18, matrix products, outer_sum(): lax.dot_general(left, right, (((0,), (0,)), ((), ())), preferred_element_...  70.1 us
    unnamed x1, blocking collectives  67.2 us
    unnamed x464, local copies, waits for them, and re-layouts  66.6 us
    dot_general x18, matrix products, back_mul(): lax.dot_general(grad_rows, matrix, (((grad_rows.ndim - 1,), (1,)), ((), (...  35.9 us
    another operation x7, local copies, waits for them, and re-layouts, one_scatter(): lines = jnp.concatenate([b.reshape(peers, -1) for b in pieces], axis=1)  27.5 us
  transfers between devices with their start and end apart: 6, of which 2 were waited for; matrix products, arithmetic and copies ran while one was open for 17% of the time, Pallas kernels for 0%

commit v1 on v0

v1 whole, which is shorter than its diff:
```python
import functools
import itertools
import math

import jax
import jax.numpy as jnp
import numpy as np
from jax import lax
from jax.experimental import pallas as pl
from jax.experimental.pallas import tpu as pltpu
from jax.sharding import Mesh
from jax.sharding import PartitionSpec as P

AX = ("zl", "c", "zh", "y", "x")
F32 = jnp.float32
BF = jnp.bfloat16
EPS = 1e-6
D, HEADS, HD, FF, WINDOW = 640, 4, 256, 2048, 512
TOK = 256
WIN = 768
ORDER = (("x", "y", "z"), ("y", "z", "x"))
NA = 64
NB = 288
N = NA + NB
INT_A, INT_B = 64, 160
RA, RB = 16 * NA, 16 * NB
DOWN_ROW, O_ROW = 2560, 3840
NP = 9472
SEG = dict(q=(0, 1024, 8, 0), kv=(1024, 512, 4, 8), o=(1536, 640, 5, 12), gate=(2176, 2048, 16, 17),
           up=(4224, 2048, 16, 33), down=(6272, 640, 5, 49))
OQ, OKV, OO, OG, OU, OD, ON = 0, 1024, 1536, 2176, 4224, 6272, 6912
U_D = 1.0 / (128.0 * math.sqrt(D))
U_O = 1.0 / (128.0 * math.sqrt(HEADS * HD))
U_F = 1.0 / (128.0 * math.sqrt(FF))
VMEM = pl.BlockSpec(memory_space=pltpu.VMEM)
SMEM = pl.BlockSpec(memory_space=pltpu.SMEM)


def lane_tables():
    lane, dev = np.zeros((1, NP), np.int32), np.zeros((1, NP), np.int32)
    for at, size, each, first in SEG.values():
        c = np.arange(size)
        lane[0, at : at + size] = first + c % each
        dev[0, at : at + size] = c // each
    for g in range(4):
        c = np.arange(D)
        at = ON + g * D
        lane[0, at : at + D] = 54 + (c % 5) * 4 + g
        dev[0, at : at + D] = c // 5
    return lane, dev


def cost_of(us):
    return pl.CostEstimate(flops=int(us * 1e6) + 1000, bytes_accessed=1000, transcendentals=0)


def call(kernel, out_shape, ins, scratch=(), mem=62, us=1, in_specs=None, name=None):
    params = dict(vmem_limit_bytes=mem << 20)
    return pl.pallas_call(
        kernel,
        out_shape=out_shape,
        in_specs=in_specs or [VMEM] * len(ins),
        out_specs=jax.tree.map(lambda s: VMEM, out_shape),
        scratch_shapes=list(scratch),
        compiler_params=pltpu.CompilerParams(**params),
        cost_estimate=cost_of(us),
        name=name,
    )(*ins)


def sds(shape, dtype):
    return jax.ShapeDtypeStruct(shape, dtype)


def dot(a, b):
    return jnp.dot(a, b, preferred_element_type=F32)


def dot_t(a, b):
    return lax.dot_general(a, b, (((1,), (1,)), ((), ())), preferred_element_type=F32)


def t_dot(a, b):
    return lax.dot_general(a, b, (((0,), (0,)), ((), ())), preferred_element_type=F32)


def flat(c, x, y, z):
    return ((((z & 1) * 2 + c) * 2 + (z >> 1)) * 4 + y) * 4 + x


@functools.lru_cache(None)
def stage_pairs(stage, r):
    pairs = []
    for c, x, y, z in itertools.product(range(2), range(4), range(4), range(4)):
        at = dict(x=x, y=y, z=z)
        axis = ORDER[c][stage]
        at[axis] = (at[axis] + r) % 4
        pairs.append((flat(c, x, y, z), flat(c, **at)))
    return tuple(sorted(pairs))


def send(a, stage, r):
    return lax.ppermute(a, AX, stage_pairs(stage, r % 4))


def behind(k):
    return [(i, i + k) for i in range(16) if i % 8 + k < 8]


def other_core(a):
    return lax.ppermute(a, "c", [(0, 1), (1, 0)])


def swap_matrix():
    row = lax.broadcasted_iota(jnp.int32, (256, 256), 0)
    col = lax.broadcasted_iota(jnp.int32, (256, 256), 1)
    return ((row % 16) * 16 + row // 16 == col).astype(BF)


BLOCKS = ((224, 80, DOWN_ROW), (304, 48, O_ROW))


def asm_kernel(*refs):
    ins, out_a, out_b = refs[:4], refs[4], refs[5]
    swap = swap_matrix()
    for g in range((INT_A + INT_B) // 16):
        x = jnp.concatenate(
            [ins[s // 4][(s % 4) * N + 16 * g : (s % 4) * N + 16 * g + 16, :] for s in range(16)], axis=0
        )
        y = dot(swap, x).astype(BF)
        if g < 4:
            out_a[256 * g : 256 * g + 256, :] = y
        else:
            out_b[256 * (g - 4) : 256 * (g - 4) + 256, :] = y
    for first, lines, row in BLOCKS:
        for s in range(16):
            at = (s % 4) * N + first
            out_b[row + s * lines : row + (s + 1) * lines, :] = ins[s // 4][at : at + lines, :]


def join_kernel(a, b, c, d, out):
    for r, ref in enumerate((a, b, c, d)):
        out[r * RA : (r + 1) * RA, :] = ref[...]


def gather(shard, tokens, early):
    one = jnp.concatenate([shard] + [send(shard, 0, r) for r in (1, 2, 3)], axis=0)
    t1, t0 = (lax.ppermute(tokens, ("y", "x"), behind(k)) for k in (1, 2))
    two = [one] + [send(one, 1, r) for r in (1, 2, 3)]
    two[0], t0, t1, *early = lax.optimization_barrier((two[0], t0, t1, *early))
    piece_a, piece_b = call(asm_kernel, [sds((RA, 128), BF), sds((RB, 128), BF)], two, name="asm", us=0)
    mine_a = [piece_a] + [send(piece_a, 2, r) for r in (1, 2, 3)]
    mine_a = call(join_kernel, sds((4 * RA, 128), BF), mine_a, name="join", us=0)
    theirs_a = other_core(mine_a)
    mine_b = [piece_b] + [send(piece_b, 2, r) for r in (1, 2, 3)]
    return mine_a, theirs_a, mine_b, other_core(piece_b), t0, t1, early


def rs1_kernel(a, b, *outs):
    for r in range(4):
        outs[r][...] = (a[r].astype(F32) + b[r].astype(F32)).astype(BF)


def total4(refs, at, rows):
    t = refs[0][at : at + rows, :].astype(F32)
    for k in (1, 2, 3):
        t = t + refs[k][at : at + rows, :].astype(F32)
    return t


def rs2_kernel(*refs):
    a, b, outs = refs[:4], refs[4:8], refs[8:]
    swap = swap_matrix()
    for g in range((INT_A + INT_B) // 16):
        t = total4(a, 256 * g, 256) if g < 4 else total4(b, 256 * (g - 4), 256)
        y = dot(swap, t.astype(BF)).astype(BF)
        for s in range(16):
            at = (s % 4) * N + 16 * g
            outs[s // 4][at : at + 16, :] = y[16 * s : 16 * s + 16]
    for first, lines, row in BLOCKS:
        for s in range(16):
            at = (s % 4) * N + first
            outs[s // 4][at : at + lines, :] = total4(b, row + s * lines, lines).astype(BF)


def rs3_kernel(*refs):
    ins, outs = refs[:4], refs[4:]
    for r in range(4):
        outs[r][...] = total4(ins, r * N, N).astype(BF)


def rs4_kernel(a0, a1, a2, a3, q, kv, gate, up, down, o, *small):
    t = total4((a0, a1, a2, a3), 0, N)
    for cb in range(8):
        q[:, cb * 128 : cb * 128 + 128] = t[cb * 5 : cb * 5 + 5]
    for cb in range(4):
        kv[:, cb * 128 : cb * 128 + 128] = t[40 + cb * 5 : 45 + cb * 5]
    at = 0
    for ref in small[:6]:
        ref[...] = t[60, at : at + ref.shape[0]]
        at += ref.shape[0]
    for j in range(5):
        small[6][j : j + 1, :] = t[60:61, at + 4 * j : at + 4 * j + 4]
    for cb in range(16):
        gate[:, cb * 128 : cb * 128 + 128] = t[64 + cb * 5 : 69 + cb * 5]
        up[:, cb * 128 : cb * 128 + 128] = t[144 + cb * 5 : 149 + cb * 5]
    for cb in range(5):
        down[:, cb * 128 : cb * 128 + 128] = t[224 + cb * 16 : 240 + cb * 16]
        o[:, cb * 128 : cb * 128 + 128] = t[304 + cb * 8 : 312 + cb * 8]


def first_hop(mine, got, rows, grid, us):
    block = rows // grid
    parts = pl.pallas_call(
        rs1_kernel,
        grid=(grid,),
        out_shape=[sds((rows, 128), BF)] * 4,
        in_specs=[pl.BlockSpec((4, block, 128), lambda i: (0, i, 0))] * 2,
        out_specs=[pl.BlockSpec((block, 128), lambda i: (i, 0))] * 4,
        compiler_params=pltpu.CompilerParams(vmem_limit_bytes=24 << 20),
        cost_estimate=cost_of(us),
        name=f"rs1_{rows}",
    )(mine.reshape(4, rows, 128), got.reshape(4, rows, 128))
    return [parts[0]] + [send(parts[r], 2, -r) for r in (1, 2, 3)]


def scatter(a, b, out_shape):
    parts = call(rs2_kernel, [sds((4 * N, 128), BF)] * 4, a + b, name="rs2", mem=24, us=0)
    parts = [parts[0]] + [send(parts[r], 1, -r) for r in (1, 2, 3)]
    parts = call(rs3_kernel, [sds((N, 128), BF)] * 4, parts, name="rs3", mem=24, us=0)
    parts = [parts[0]] + [send(parts[r], 0, -r) for r in (1, 2, 3)]
    return call(rs4_kernel, out_shape, parts, name="rs4", mem=24, us=0)


def pack_kernel(q, kv, o, gate, up, down, sq, skv, so, sg, su, sd, gains, out, wide):
    for cb in range(8):
        wide[cb * 5 : cb * 5 + 5, :] = q[:, cb * 128 : cb * 128 + 128].astype(F32)
    for cb in range(4):
        wide[40 + cb * 5 : 45 + cb * 5, :] = kv[:, cb * 128 : cb * 128 + 128].astype(F32)
    row = [ref[...].reshape(1, -1) for ref in (sq, skv, so, sg, su, sd)] + [gains[j : j + 1, :] for j in range(5)]
    v = jnp.concatenate(row + [jnp.zeros((1, 54), F32)], axis=1)
    hi = v.astype(BF).astype(F32)
    mid = (v - hi).astype(BF).astype(F32)
    wide[60:61, :] = hi
    wide[61:62, :] = mid
    wide[62:63, :] = v - hi - mid
    wide[63:64, :] = jnp.zeros((1, 128), F32)
    for cb in range(16):
        wide[64 + cb * 5 : 69 + cb * 5, :] = gate[:, cb * 128 : cb * 128 + 128].astype(F32)
        wide[144 + cb * 5 : 149 + cb * 5, :] = up[:, cb * 128 : cb * 128 + 128].astype(F32)
    for cb in range(5):
        wide[224 + cb * 16 : 240 + cb * 16, :] = down[:, cb * 128 : cb * 128 + 128].astype(F32)
        wide[304 + cb * 8 : 312 + cb * 8, :] = o[:, cb * 128 : cb * 128 + 128].astype(F32)
    wide[344:352, :] = jnp.zeros((8, 128), F32)
    out[...] = wide[...].astype(BF)


def piece(mine, theirs, p, rows):
    return (mine if p < 4 else theirs), (p % 4) * rows


def perm_matrix(dk):
    return (lax.broadcasted_iota(jnp.int32, (D, D), 0) == dk).astype(BF)


def steps_of(b):
    step = jnp.where(b == 0, 1.0, jnp.where(b == 1, 16.0, 64.0)).astype(F32)
    inv = jnp.where(b == 0, 1.0, jnp.where(b == 1, 1.0 / 16, 1.0 / 64)).astype(F32)
    return step, inv


def level_maker(b, rows=16, dtype=BF):
    step, inv = steps_of(b)
    step_v = jnp.full((rows, 128), step, F32)
    inv_v = jnp.full((rows, 128), inv, F32).astype(dtype)
    half_v = (step_v * 0.5).astype(dtype)
    step_v = step_v.astype(dtype)
    return lambda c: jnp.floor(c * inv_v) * step_v + half_v


def dequant_a(b, mine, theirs, lq, lkv):
    level = level_maker(b)
    for p in range(8):
        ref, base = piece(mine, theirs, p, RA)
        for j in range(5):
            for cb in range(8):
                at = base + (cb * 5 + j) * 16
                lq[j * 128 + p * 16 : j * 128 + p * 16 + 16, cb * 128 : cb * 128 + 128] = level(ref[at : at + 16, :])
            for cb in range(4):
                at = base + (40 + cb * 5 + j) * 16
                lkv[j * 128 + p * 16 : j * 128 + p * 16 + 16, cb * 128 : cb * 128 + 128] = level(ref[at : at + 16, :])


def make_mask(segq, segk, mask):
    for t in range(2):
        r = lax.broadcasted_iota(jnp.int32, (128, 640), 0)
        c = lax.broadcasted_iota(jnp.int32, (128, 640), 1)
        ok = (c <= WINDOW + r) & (c > r)
        ok = ok & (segq[t * 128 : t * 128 + 128, :] == segk[:, t * 128 : t * 128 + 640])
        mask[t] = ok.astype(F32)


def rope(v, cos, sin):
    a, b = v[:, :128], v[:, 128:]
    return jnp.concatenate([a * cos - b * sin, b * cos + a * sin], axis=1)


def unrope(v, cos, sin):
    a, b = v[:, :128], v[:, 128:]
    return jnp.concatenate([a * cos + b * sin, b * cos - a * sin], axis=1)


TANH_IN = 1.0 / (16.0 * 50.0)
EXP2_IN = 50.0 * math.log2(math.e)


def first_kernel(
    run, mine, theirs, dev_col, lane_of, dev_of, t0, t1, t2, dk, cos, sin, segq, segk,
    par, h1p, q_out, kv_out, mix_out, lq, lkv, mask, sc, ex, tot,
):
    lines = []
    for l in (60, 61, 62):
        refs = [piece(mine, theirs, p, RA) for p in range(8)]
        lines.append(jnp.concatenate([ref[at + l * 16 : at + l * 16 + 16, :] for ref, at in refs], axis=0))
    lines = jnp.concatenate(lines, axis=1)
    devs = dev_col[...]
    row = lax.broadcasted_iota(jnp.int32, (128, 256), 0)
    for i in range(NP // 256):
        cols = slice(i * 256, i * 256 + 256)
        one_hot = (row == lane_of[:, cols]).astype(BF)
        t = dot(lines, jnp.concatenate([one_hot] * 3, axis=0))
        t = jnp.where(devs == dev_of[:, cols], t, 0.0)
        par[:, cols] = jnp.sum(t, axis=0, keepdims=True)
    perm = perm_matrix(dk[...])
    gain = par[:, ON : ON + D]
    for k, t in enumerate((t0, t1, t2)):
        v = t[...].astype(F32)
        h = v * lax.rsqrt(jnp.mean(v * v, axis=-1, keepdims=True) + EPS) * gain
        h1p[k * 256 : k * 256 + 256, :] = dot(h.astype(BF), perm).astype(BF)
    make_mask(segq, segk, mask)

    def width(b, carry):
        @pl.when(run[b] == 0)
        def _():
            mix_out[b] = jnp.zeros((TOK, HEADS * HD), BF)

        @pl.when(run[b] > 0)
        def _():
            dequant_a(b, mine, theirs, lq, lkv)
            own = h1p[512:768, :]
            co, so = cos[512:768, :], sin[512:768, :]
            for h in range(4):
                scale = par[:, OQ + h * 256 : OQ + h * 256 + 256] * U_D
                q = rope(dot(own, lq[:, h * 256 : h * 256 + 256]) * scale, co, so).astype(BF)
                for t in range(2):
                    q_out[b, t, h * 128 : h * 128 + 128, :] = q[t * 128 : t * 128 + 128]
            for k in range(3):
                rows = h1p[k * 256 : k * 256 + 256, :]
                cw, sw = cos[k * 256 : k * 256 + 256, :], sin[k * 256 : k * 256 + 256, :]
                key = dot(rows, lkv[:, :256]) * (par[:, OKV : OKV + 256] * U_D)
                kv_out[b, k * 256 : k * 256 + 256, 0:256] = rope(key, cw, sw).astype(BF)
                val = dot(rows, lkv[:, 256:]) * (par[:, OKV + 256 : OKV + 512] * U_D)
                kv_out[b, k * 256 : k * 256 + 256, 256:512] = val.astype(BF)
            for t in range(2):
                keys = kv_out[b, t * 128 : t * 128 + 640, 0:256]
                vals = kv_out[b, t * 128 : t * 128 + 640, 256:512]
                sc[...] = dot_t(q_out[b, t], keys)

                def soft(i, carry):
                    at = pl.multiple_of(i * 32, 32)
                    m = mask[t, pl.ds(pl.multiple_of((i % 4) * 32, 32), 32), :]
                    e = jnp.exp2(jnp.tanh(sc[pl.ds(at, 32), :] * TANH_IN) * EXP2_IN) * m
                    tot[pl.ds(at, 32), :] = jnp.broadcast_to(1.0 / jnp.sum(e, axis=1, keepdims=True), (32, 128))
                    ex[pl.ds(at, 32), :] = e.astype(BF)
                    return carry

                lax.fori_loop(0, 16, soft, 0, unroll=4)
                mixed = dot(ex[...], vals) * tot[:, 0:1]
                for h in range(4):
                    mix_out[b, t * 128 : t * 128 + 128, h * 256 : h * 256 + 256] = mixed[h * 128 : h * 128 + 128].astype(BF)

        return carry

    lax.fori_loop(0, 3, width, 0)


def mean_of(v):
    return jnp.mean(v, axis=-1, keepdims=True)


C_G = math.sqrt(2.0 / math.pi)
C_3 = C_G * 0.044715
PARTS = ((O_ROW, 768), (0, 2560), (DOWN_ROW, 1280))


def middle_kernel(
    run, inat, mix, tok, cot, b0, b1, b2, b3, b4, b5, b6, b7, par, dk,
    out, rest, gmix, g_mine, g_theirs, gpar,
    pcs, lgu, ld, lo, onat, gu32, gate, up, aa, bb, hid, gg, gu, h2s, gbr, gat, att, mid, acc, perm, outv,
    in_sem, gu_sem, do_sem, out_sem,
):
    dwd, dwo = ld, onat
    loads = [
        [
            pltpu.make_async_copy(ref.at[pl.ds(first, rows)], pcs.at[p, pl.ds(first, rows)], in_sem.at[k, p])
            for p, ref in enumerate((b0, b1, b2, b3, b4, b5, b6, b7))
        ]
        for k, (first, rows) in enumerate(PARTS)
    ]
    for group in loads:
        for copy in group:
            copy.start()
    perm[...] = perm_matrix(dk[...])
    rest[...] = jnp.zeros_like(rest)
    gpar[...] = jnp.zeros_like(gpar)
    for copy in loads[0]:
        copy.wait()
    for p in range(8):
        for s in range(16):
            at = O_ROW + s * 48
            block = pcs[p, at : at + 48, :].astype(F32)
            row = pl.multiple_of(inat[p * 16 + s] * 8, 8)
            for cb in range(5):
                onat[pl.ds(row, 8), cb * 128 : cb * 128 + 128] = block[cb * 8 : cb * 8 + 8]
    for copy in loads[1] + loads[2]:
        copy.wait()

    def width(b, carry):
        rows = pl.ds(pl.multiple_of(b * TOK, TOK), TOK)

        @pl.when(run[b] == 0)
        def _():
            outv[b] = jnp.zeros((TOK, D), F32)
            hid[rows, :] = jnp.zeros((TOK, FF), BF)
            gg[rows, :] = jnp.zeros((TOK, FF), BF)
            gu[rows, :] = jnp.zeros((TOK, FF), BF)
            h2s[rows, :] = jnp.zeros((TOK, D), BF)
            gbr[rows, :] = jnp.zeros((TOK, D), BF)
            gat[rows, :] = jnp.zeros((TOK, D), BF)

        @pl.when(run[b] > 0)
        def _():
            level = level_maker(b)
            wide = level_maker(b, 8, F32)
            for r in range(64):
                for cb in range(5):
                    two = [wide(onat[r * 16 + k * 8 : r * 16 + k * 8 + 8, cb * 128 : cb * 128 + 128]) for k in (0, 1)]
                    lo[r * 16 : r * 16 + 16, cb * 128 : cb * 128 + 128] = jnp.concatenate(two, axis=0).astype(BF)
            s_o = par[:, OO : OO + D] * U_O
            s_d = par[:, OD : OD + D] * U_F
            g1, g2, g3 = (par[:, ON + k * D : ON + (k + 1) * D] for k in (1, 2, 3))
            attended = dot(mix[b], lo[...]) * s_o
            att[...] = attended
            r1 = lax.rsqrt(mean_of(attended * attended) + EPS)
            middle = tok[...].astype(F32) + attended * r1 * g1
            mid[...] = middle
            r2 = lax.rsqrt(mean_of(middle * middle) + EPS)
            h2 = (middle * r2 * g2).astype(BF)
            h2p = dot(h2, perm[...]).astype(BF)
            h2s[rows, :] = h2p

            def gate_up(f):
                for half in range(2):
                    cb = f * 2 + half
                    for first, to in ((0, f * 512), (80, f * 512 + 256)):
                        for j in range(5):
                            for p in range(8):
                                at = (first + cb * 5 + j) * 16
                                k = j * 128 + p * 16
                                col = to + half * 128
                                lgu[k : k + 16, col : col + 128] = level(pcs[p, at : at + 16, :])
                gu32[f % 2] = dot(h2p, lgu[:, f * 512 : f * 512 + 512])

            gate_up(0)
            for p in range(8):
                for s in range(16):
                    row = pl.multiple_of(inat[p * 16 + s] * 16, 16)
                    for cb in range(5):
                        at = DOWN_ROW + s * 80 + cb * 16
                        ld[pl.ds(row, 16), cb * 128 : cb * 128 + 128] = level(pcs[p, at : at + 16, :])
            for f in range(8):
                if f < 7:
                    gate_up(f + 1)
                cols = slice(f * 256, f * 256 + 256)
                s_g, s_u = par[:, OG + f * 256 : OG + f * 256 + 256] * U_D, par[:, OU + f * 256 : OU + f * 256 + 256] * U_D
                parts = []
                for rc in range(8):
                    rr = slice(rc * 32, rc * 32 + 32)
                    x = gu32[f % 2, rr, 0:256] * s_g
                    u = gu32[f % 2, rr, 256:512] * s_u
                    gate[rr, cols] = x.astype(BF)
                    up[rr, cols] = u.astype(BF)
                    x2 = x * x
                    hf = 0.5 * jnp.tanh(x * (C_G + C_3 * x2)) + 0.5
                    gl = x * hf
                    aa[rr, cols] = u * (hf + (gl - gl * hf) * (2 * C_G + (6 * C_3) * x2))
                    bb[rr, cols] = gl
                    parts.append((gl * u).astype(BF))
                h = jnp.concatenate(parts, axis=0)
                hid[rows, cols] = h
                add = dot(h, ld[cols, :])
                acc[...] = add if f == 0 else acc[...] + add
            branch = acc[...] * s_d
            r3 = lax.rsqrt(mean_of(branch * branch) + EPS)
            outv[b] = mid[...] + branch * r3 * g3
            gy = cot[b].astype(F32)
            gpar[:, ON + 3 * D : ON + 4 * D] += jnp.sum(gy * branch * r3, axis=0, keepdims=True)
            w = g3 * gy
            gb = r3 * w - branch * (r3 * r3 * r3 * mean_of(w * branch))
            gpar[:, OD : OD + D] += jnp.sum(gb * branch, axis=0, keepdims=True)
            gb = (gb * s_d).astype(BF)
            gbr[rows, :] = gb

            def grad_hidden(f):
                gu32[f % 2, :, 0:256] = dot_t(gb, ld[f * 256 : f * 256 + 256, :])

            ones = jnp.ones((8, TOK), BF)
            grad_hidden(0)
            for f in range(8):
                if f < 7:
                    grad_hidden(f + 1)
                cols = slice(f * 256, f * 256 + 256)
                col_g, col_u = slice(OG + f * 256, OG + f * 256 + 256), slice(OU + f * 256, OU + f * 256 + 256)
                s_g, s_u = par[:, col_g] * U_D, par[:, col_u] * U_D
                parts, prods = [], []
                for rc in range(8):
                    rr = slice(rc * 32, rc * 32 + 32)
                    g = gu32[f % 2, rr, 0:256]
                    gg_b = (g * aa[rr, cols] * s_g).astype(BF)
                    gu_b = (g * bb[rr, cols] * s_u).astype(BF)
                    parts.append(jnp.concatenate([gg_b, gu_b], axis=1))
                    prods.append(jnp.concatenate([gg_b * gate[rr, cols], gu_b * up[rr, cols]], axis=1))
                both = jnp.concatenate(parts, axis=0)
                gg[rows, cols] = both[:, 0:256]
                gu[rows, cols] = both[:, 256:512]
                sums = dot(ones, jnp.concatenate(prods, axis=0))
                gpar[:, col_g] += sums[0:1, 0:256]
                gpar[:, col_u] += sums[0:1, 256:512]
                add = dot_t(both, lgu[:, f * 512 : f * 512 + 512])
                acc[...] = add if f == 0 else acc[...] + add
            g_h2 = acc[...]
            high = g_h2.astype(BF)
            low = (g_h2 - high.astype(F32)).astype(BF)
            g_h2 = dot_t(high, perm[...]) + dot_t(low, perm[...])
            middle = mid[...]
            attended = att[...]
            gpar[:, ON + 2 * D : ON + 3 * D] += jnp.sum(g_h2 * middle * r2, axis=0, keepdims=True)
            w = g2 * g_h2
            gmid = cot[b].astype(F32) + r2 * w - middle * (r2 * r2 * r2 * mean_of(w * middle))
            rest[...] += gmid
            gpar[:, ON + D : ON + 2 * D] += jnp.sum(gmid * attended * r1, axis=0, keepdims=True)
            w = g1 * gmid
            ga = r1 * w - attended * (r1 * r1 * r1 * mean_of(w * attended))
            gpar[:, OO : OO + D] += jnp.sum(ga * attended, axis=0, keepdims=True)
            ga = (ga * s_o).astype(BF)
            gat[rows, :] = ga
            gmix[b] = dot_t(ga, lo[...]).astype(BF)

        return carry

    lax.fori_loop(0, 3, width, 0)
    out_copy = pltpu.make_async_copy(outv, out, out_sem)
    out_copy.start()
    gpar[:, OO : OO + D] = gpar[:, OO : OO + D] / par[:, OO : OO + D]
    for at in (OG, OU):
        scale = par[:, at : at + FF]
        gpar[:, at : at + FF] = gpar[:, at : at + FF] / (scale * scale * U_D)
    gpar[:, OD : OD + D] = gpar[:, OD : OD + D] / par[:, OD : OD + D]

    stores = []

    def leave(p, first, rows, sem):
        to, base = piece(g_mine, g_theirs, p, RB)
        copy = pltpu.make_async_copy(pcs.at[p, pl.ds(first, rows)], to.at[pl.ds(base + first, rows)], sem)
        copy.start()
        stores.append(copy)

    g_all = gbr[...]
    for f in range(8):
        cols = slice(f * 256, f * 256 + 256)
        dwd[cols, :] = t_dot(hid[:, cols], g_all).astype(BF)
    for p in range(8):
        for s in range(16):
            row = pl.multiple_of(inat[p * 16 + s] * 16, 16)
            for cb in range(5):
                at = DOWN_ROW + s * 80 + cb * 16
                pcs[p, at : at + 16, :] = dwd[pl.ds(row, 16), cb * 128 : cb * 128 + 128]
        leave(p, DOWN_ROW, 1280, do_sem.at[0, p])
    for h in range(4):
        w = jnp.zeros((256, D), F32)
        for b in range(3):
            w = w + t_dot(mix[b, :, h * 256 : h * 256 + 256], gat[b * TOK : (b + 1) * TOK, :])
        dwo[h * 256 : h * 256 + 256, :] = w
    for p in range(8):
        for s in range(16):
            row = pl.multiple_of(inat[p * 16 + s] * 8, 8)
            parts = [dwo[pl.ds(row, 8), cb * 128 : cb * 128 + 128] for cb in range(5)] + [jnp.zeros((8, 128), F32)]
            at = O_ROW + s * 48
            pcs[p, at : at + 48, :] = jnp.concatenate(parts, axis=0).astype(BF)
        leave(p, O_ROW, 768, do_sem.at[1, p])
    h2t = h2s[...]
    for f in range(8):
        cols = slice(f * 256, f * 256 + 256)
        for k, (first, ref) in enumerate(((0, gg), (80, gu))):
            w = t_dot(h2t, ref[:, cols]).astype(BF)
            for half in range(2):
                for j in range(5):
                    for p in range(8):
                        at = (first + (f * 2 + half) * 5 + j) * 16
                        r = j * 128 + p * 16
                        pcs[p, at : at + 16, :] = w[r : r + 16, half * 128 : half * 128 + 128]
            if f % 2:
                for p in range(8):
                    leave(p, (first + (f - 1) * 10) * 16, 320, gu_sem.at[f // 2, k, p])
    for copy in stores:
        copy.wait()
    out_copy.wait()


def attn_back_kernel(
    first, count, run, par, cos, sin, segq, segk, q, kv, gmix, gpar2,
    gqb, gkvb, gpar,
    mask, sc, gp, pb, gz, gq, gkv,
):
    make_mask(segq, segk, mask)
    gpar[...] = gpar2[...]

    def width(k, carry):
        b = first + k
        @pl.when(run[b] > 0)
        def _():
            gkv[...] = jnp.zeros_like(gkv)
            for t in range(2):
                win = slice(t * 128, t * 128 + 640)
                keys = kv[b, win, 0:256]
                vals = kv[b, win, 256:512]
                gm = jnp.concatenate(
                    [gmix[b, t * 128 : t * 128 + 128, h * 256 : h * 256 + 256] for h in range(4)], axis=0
                )
                sc[...] = dot_t(q[b, t], keys)
                gp[...] = dot_t(gm, vals)

                def soft(i, carry):
                    at = pl.multiple_of(i * 16, 16)
                    m = mask[t, pl.ds(pl.multiple_of((i % 8) * 16, 16), 16), :]
                    th = jnp.tanh(sc[pl.ds(at, 16), :] * TANH_IN)
                    e = jnp.exp2(th * EXP2_IN) * m
                    p = e * (1.0 / jnp.sum(e, axis=1, keepdims=True))
                    pb[pl.ds(at, 16), :] = p.astype(BF)
                    pg = p * gp[pl.ds(at, 16), :]
                    dd = jnp.sum(pg, axis=1, keepdims=True)
                    gz[pl.ds(at, 16), :] = ((pg - p * dd) * (1.0 - th * th)).astype(BF)
                    return carry

                lax.fori_loop(0, 32, soft, 0, unroll=4)
                gkv[win, 256:512] += t_dot(pb[...], gm)
                gkv[win, 0:256] += t_dot(gz[...], q[b, t]) * (1.0 / 16)
                gq[t] = dot(gz[...], keys) * (1.0 / 16)
            co, so = cos[512:768, :], sin[512:768, :]
            for h in range(4):
                cols = slice(h * 256, h * 256 + 256)
                g = unrope(jnp.concatenate([gq[t, h * 128 : h * 128 + 128, :] for t in (0, 1)], axis=0), co, so)
                raw = jnp.concatenate([q[b, t, h * 128 : h * 128 + 128, :] for t in (0, 1)], axis=0)
                raw = unrope(raw.astype(F32), co, so)
                gpar[:, OQ + h * 256 : OQ + h * 256 + 256] += jnp.sum(g * raw, axis=0, keepdims=True)
                g = g * (par[:, OQ + h * 256 : OQ + h * 256 + 256] * U_D)
                gqb[k, :, cols] = g.astype(BF)
            for w in range(3):
                rows = slice(w * 256, w * 256 + 256)
                cw, sw = cos[rows, :], sin[rows, :]
                for half in range(2):
                    cols = slice(half * 256, half * 256 + 256)
                    g = gkv[rows, cols]
                    raw = kv[b, rows, cols].astype(F32)
                    if half == 0:
                        g, raw = unrope(g, cw, sw), unrope(raw, cw, sw)
                    at = OKV + half * 256
                    gpar[:, at : at + 256] += jnp.sum(g * raw, axis=0, keepdims=True)
                    g = g * (par[:, at : at + 256] * U_D)
                    gkvb[k, rows, cols] = g.astype(BF)

        return carry

    lax.fori_loop(0, count, width, 0)


def last_kernel(
    run, h1p, mine, theirs, gqb0, gkvb0, gqb1, gkvb1, par, gpar_in, dk, dev_col, lane_of, dev_of, t0, t1, t2,
    own, back1, back2, g_mine, g_theirs,
    lq, lkv, gh1, gpar, gq_sum, gkv_sum, gqs, gkvs,
):
    gh1[...] = jnp.zeros_like(gh1)
    gpar[...] = gpar_in[...]
    gpar[:, OQ : OQ + 1536] = gpar[:, OQ : OQ + 1536] / par[:, OQ : OQ + 1536]
    gq_sum[...] = jnp.zeros_like(gq_sum)
    gkv_sum[...] = jnp.zeros_like(gkv_sum)
    for b, (gqb, gkvb, at) in enumerate(((gqb0, gkvb0, 0), (gqb1, gkvb1, 0), (gqb1, gkvb1, 1))):

        @pl.when(run[b] > 0)
        def _(gqb=gqb, gkvb=gkvb, at=at):
            gq_sum[...] += gqb[at].astype(F32)
            gkv_sum[...] += gkvb[at].astype(F32)

    gqs[...] = gq_sum[...].astype(BF)
    gkvs[...] = gkv_sum[...].astype(BF)

    def put(w, first):
        for half in range(2):
            for j in range(5):
                for p in range(8):
                    to, base = piece(g_mine, g_theirs, p, RA)
                    at = base + (first + half * 5 + j) * 16
                    k = j * 128 + p * 16
                    to[at : at + 16, :] = w[k : k + 16, half * 128 : half * 128 + 128]

    for f in range(4):
        put(t_dot(h1p[512:768, :], gqs[:, f * 256 : f * 256 + 256]).astype(BF), f * 10)
    for f in range(2):
        put(t_dot(h1p[...], gkvs[:, f * 256 : f * 256 + 256]).astype(BF), 40 + f * 10)

    for b, (gqb, gkvb, at) in enumerate(((gqb0, gkvb0, 0), (gqb1, gkvb1, 0), (gqb1, gkvb1, 1))):

        @pl.when(run[b] > 0)
        def _(b=b, gqb=gqb, gkvb=gkvb, at=at):
            dequant_a(b, mine, theirs, lq, lkv)
            gh1[512:768, :] += dot_t(gqb[at], lq[...])
            for k in range(3):
                gh1[k * 256 : k * 256 + 256, :] += dot_t(gkvb[at, k * 256 : k * 256 + 256, :], lkv[...])

    perm = perm_matrix(dk[...])
    gain_sum = jnp.zeros((1, D), F32)
    for k, (t, to) in enumerate(((t0, back2), (t1, back1), (t2, own))):
        g = gh1[k * 256 : k * 256 + 256, :]
        high = g.astype(BF)
        low = (g - high.astype(F32)).astype(BF)
        g = dot_t(high, perm) + dot_t(low, perm)
        v = t[...].astype(F32)
        r = lax.rsqrt(mean_of(v * v) + EPS)
        gain_sum = gain_sum + jnp.sum(g * v * r, axis=0, keepdims=True)
        to[...] = g.astype(to.dtype)
    gpar[:, ON : ON + D] = gain_sum

    devs = dev_col[...]
    sums = jnp.zeros((128, 128), F32)
    row = lax.broadcasted_iota(jnp.int32, (128, 256), 0)
    for i in range(NP // 256):
        cols = slice(i * 256, i * 256 + 256)
        one_hot = (row == lane_of[:, cols]).astype(BF)
        sums = sums + dot_t(jnp.where(devs == dev_of[:, cols], gpar[:, cols], 0.0).astype(BF), one_hot)
    sums = sums.astype(BF)
    for p in range(8):
        to, base = piece(g_mine, g_theirs, p, RA)
        to[base + 960 : base + 976, :] = sums[p * 16 : p * 16 + 16]
        to[base + 976 : base + 1024, :] = jnp.zeros((48, 128), BF)


def end_kernel(own, got1, got2, tok, rest, par, out):
    g = own[...] + got1[...].astype(F32) + got2[...].astype(F32)
    v = tok[...].astype(F32)
    r = lax.rsqrt(mean_of(v * v) + EPS)
    w = par[:, ON : ON + D] * g
    out[...] = rest[...] + r * w - v * (r * r * r * mean_of(w * v))


def run_first(args):
    return call(
        first_kernel,
        [
            sds((1, NP), F32), sds((WIN, D), BF),
            sds((3, 2, 512, HD), BF), sds((3, WIN, 2 * HD), BF), sds((3, TOK, HEADS * HD), BF),
        ],
        args,
        scratch=[
            pltpu.VMEM((D, 1024), BF), pltpu.VMEM((D, 512), BF), pltpu.VMEM((2, 128, 640), F32),
            pltpu.VMEM((512, 640), F32), pltpu.VMEM((512, 640), BF), pltpu.VMEM((512, 128), F32),
        ],
        in_specs=[SMEM] + [VMEM] * 13, name="first", us=20,
    )


def run_middle(args):
    out_shape = [
        sds((3, TOK, D), F32), sds((TOK, D), F32), sds((3, TOK, HEADS * HD), BF),
        sds((4 * RB, 128), BF), sds((4 * RB, 128), BF), sds((1, NP), F32),
    ]
    any_ = pl.BlockSpec(memory_space=pl.ANY)
    return pl.pallas_call(
        middle_kernel,
        out_shape=out_shape,
        in_specs=[SMEM, SMEM] + [VMEM] * 3 + [any_] * 8 + [VMEM] * 2,
        out_specs=[any_, VMEM, VMEM, any_, any_, VMEM],
        scratch_shapes=[
            pltpu.VMEM((8, RB, 128), BF), pltpu.VMEM((D, 2 * FF), BF), pltpu.VMEM((FF, D), BF), pltpu.VMEM((1024, D), BF),
            pltpu.VMEM((1024, D), F32), pltpu.VMEM((2, TOK, 512), F32),
            pltpu.VMEM((TOK, FF), BF), pltpu.VMEM((TOK, FF), BF), pltpu.VMEM((TOK, FF), F32), pltpu.VMEM((TOK, FF), F32),
            pltpu.VMEM((3 * TOK, FF), BF), pltpu.VMEM((3 * TOK, FF), BF), pltpu.VMEM((3 * TOK, FF), BF),
            pltpu.VMEM((3 * TOK, D), BF), pltpu.VMEM((3 * TOK, D), BF), pltpu.VMEM((3 * TOK, D), BF),
            pltpu.VMEM((TOK, D), F32), pltpu.VMEM((TOK, D), F32), pltpu.VMEM((TOK, D), F32),
            pltpu.VMEM((D, D), BF), pltpu.VMEM((3, TOK, D), F32),
            pltpu.SemaphoreType.DMA((3, 8)), pltpu.SemaphoreType.DMA((4, 2, 8)), pltpu.SemaphoreType.DMA((2, 8)),
            pltpu.SemaphoreType.DMA,
        ],
        compiler_params=pltpu.CompilerParams(vmem_limit_bytes=62 << 20),
        cost_estimate=cost_of(70),
        name="middle",
    )(*args)


def run_attnb(first, count, args):
    return call(
        functools.partial(attn_back_kernel, first, count),
        [sds((count, TOK, 1024), BF), sds((count, WIN, 512), BF), sds((1, NP), F32)],
        args,
        scratch=[
            pltpu.VMEM((2, 128, 640), F32), pltpu.VMEM((512, 640), F32), pltpu.VMEM((512, 640), F32),
            pltpu.VMEM((512, 640), BF), pltpu.VMEM((512, 640), BF),
            pltpu.VMEM((2, 512, HD), F32), pltpu.VMEM((WIN, 512), F32),
        ],
        in_specs=[SMEM] + [VMEM] * 9, mem=28, name=f"attnb{first}", us=8 * count,
    )


def run_last(args):
    return call(
        last_kernel,
        [
            sds((TOK, D), F32), sds((TOK, D), BF), sds((TOK, D), BF),
            sds((4 * RA, 128), BF), sds((4 * RA, 128), BF),
        ],
        args,
        scratch=[
            pltpu.VMEM((D, 1024), BF), pltpu.VMEM((D, 512), BF),
            pltpu.VMEM((WIN, D), F32), pltpu.VMEM((1, NP), F32),
            pltpu.VMEM((TOK, 1024), F32), pltpu.VMEM((WIN, 512), F32), pltpu.VMEM((TOK, 1024), BF), pltpu.VMEM((WIN, 512), BF),
        ],
        in_specs=[SMEM] + [VMEM] * 16, mem=28, name="last", us=14,
    )


def per_device(
    tokens, cotangent, segment_ids, width_mask,
    q_codes, kv_codes, o_codes, gate_codes, up_codes, down_codes,
    q_scale, kv_scale, o_scale, gate_scale, up_scale, down_scale, norm_gains,
):
    c, x, y = lax.axis_index("c"), lax.axis_index("x"), lax.axis_index("y")
    zl, zh = lax.axis_index("zl"), lax.axis_index("zh")
    z = zh * 2 + zl
    lane_of, dev_of = lane_tables()

    p, s = jnp.arange(128, dtype=jnp.int32) // 16, jnp.arange(128, dtype=jnp.int32) % 16
    shift = (s % 4, s // 4, p % 4)
    core = jnp.where(p < 4, c, 1 - c)
    sx, sy, sz = (
        (at - jnp.where(core == 0, shift[ORDER[0].index(a)], shift[ORDER[1].index(a)])) % 4 for at, a in ((x, "x"), (y, "y"), (z, "z"))
    )
    inat = ((((sz % 2) * 2 + core) * 2 + sz // 2) * 4 + sy) * 4 + sx
    dk = (5 * inat[None, :] + jnp.arange(5, dtype=jnp.int32)[:, None]).reshape(1, D)
    dev_col = inat[:, None]

    place = (y % 2) * 4 + x
    seq = zh * 2 + y // 2
    segs = lax.dynamic_slice_in_dim(segment_ids, seq, 1, 0)
    run = lax.dynamic_slice_in_dim(width_mask, seq, 1, 0)[0]
    padded = jnp.concatenate([jnp.full((1, WINDOW), -1, jnp.int32), segs], axis=1)
    segk = lax.dynamic_slice_in_dim(padded, place * TOK, WIN, 1)
    segq = segk[0, WINDOW:][:, None]
    pos = (place * TOK - WINDOW + jnp.arange(WIN, dtype=jnp.int32)).astype(F32)
    inverse = 10000.0 ** (-2.0 * jnp.arange(HD // 2).astype(F32) / HD)
    angles = pos[:, None] * inverse[None, :]
    cos, sin = jnp.cos(angles), jnp.sin(angles)

    shard = call(
        pack_kernel, sds((N, 128), BF),
        (q_codes, kv_codes, o_codes, gate_codes, up_codes, down_codes, q_scale, kv_scale, o_scale, gate_scale, up_scale, down_scale, norm_gains),
        scratch=[pltpu.VMEM((N, 128), F32)], name="pack", us=0,
    )
    early = (run, inat, dk, dev_col, segq, segk, cos, sin)
    mine_a, theirs_a, mine_b, their_first, t0, t1, early = gather(shard, tokens, early)
    run, inat, dk, dev_col, segq, segk, cos, sin = early

    par, h1p, q, kv, mix = run_first((run, mine_a, theirs_a, dev_col, lane_of, dev_of, t0, t1, tokens, dk, cos, sin, segq, segk))
    mix, *late = lax.optimization_barrier((mix, *mine_b[1:]))
    pieces_b = [mine_b[0], *late, their_first] + [other_core(b) for b in late]
    out, rest, gmix, gm_b, gt_b, gpar = run_middle((run, inat, mix, tokens, cotangent, *pieces_b, par, dk))
    got_b = other_core(gt_b)
    gqb, gkvb = [], []
    for first, count in ((0, 1), (1, 2)):
        got = run_attnb(first, count, (run, par, cos, sin, segq, segk, q, kv, gmix, gpar))
        gqb.append(got[0])
        gkvb.append(got[1])
        gpar = got[2]
        if first == 0:
            gpar, got_b = lax.optimization_barrier((gpar, got_b))
            parts_b = first_hop(gm_b, got_b, RB, 2, 0)
            gpar, parts_b[0] = lax.optimization_barrier((gpar, parts_b[0]))
    own, back1, back2, gm_a, gt_a = run_last(
        (run, h1p, mine_a, theirs_a, gqb[0], gkvb[0], gqb[1], gkvb[1], par, gpar, dk, dev_col, lane_of, dev_of, t0, t1, tokens)
    )
    gt_a, *parts_b = lax.optimization_barrier((gt_a, *parts_b))
    parts_a = first_hop(gm_a, other_core(gt_a), RA, 1, 0)
    gq, gkv, gate, up, down, o, *small = scatter(
        parts_a, parts_b,
        [sds((5, 1024), F32), sds((5, 512), F32), sds((5, FF), F32), sds((5, FF), F32), sds((16, D), F32), sds((8, D), F32),
         sds((8,), F32), sds((4,), F32), sds((5,), F32), sds((16,), F32), sds((16,), F32), sds((5,), F32), sds((5, 4), F32)],
    )
    forth = lambda k: [(j, i) for i, j in behind(k)]
    got1 = lax.ppermute(back1, ("y", "x"), forth(1))
    got2 = lax.ppermute(back2, ("y", "x"), forth(2))
    grad_tokens = call(end_kernel, sds((TOK, D), F32), (own, got1, got2, tokens, rest, par), name="end", mem=24, us=0)

    return (out, grad_tokens, gq, gkv, o, gate, up, down, *small)


def solution(mesh):
    fine = Mesh(mesh.devices.reshape(2, 2, 2, 4, 4), AX)
    rows, seqs = P(AX, None), P(("zl", "c"), None)
    wide = P(None, AX, None)
    return jax.shard_map(
        per_device,
        mesh=fine,
        in_specs=(rows, wide, seqs, seqs) + (rows,) * 6 + (P(AX),) * 6 + (rows,),
        out_specs=(wide, rows) + (rows,) * 6 + (P(AX),) * 6 + (rows,),
        check_vma=False,
    )
```

time: 1250 us -> 245 us (0.20)
  blocking collectives: 390 us -> 0 us
  local copies, waits for them, and re-layouts: 266 us -> 14.6 us
  matrix products: 215 us -> 0 us
  waiting for transfers between devices: 257 us -> 49.2 us
  Pallas kernels: 0 us -> 94.6 us
  other arithmetic: 72.9 us -> 4.78 us
  starting transfers between devices: 20.1 us -> 75.7 us
  between operations: 19.1 us -> 1.63 us
    all_gather x1 -> x0, blocking collectives: 323 us -> none  [side_by_side(): out, at, done = (lax.all_gather(both, axis, axis=dim, tiled=True), 0, [])]
    unnamed x3 -> x0, waiting for transfers between devices: 250 us -> none
    dot_general x72 -> x0, matrix products: 215 us -> none  [the longest x18 70.1 us: outer_sum(): lax.dot_general(left, right, (((0,), (0,)), ((), ())), preferred_element_...]
    pallas_call x0 -> x14, Pallas kernels: none -> 94.6 us  [the longest x11 50.5 us: call(): pl.pallas_call(kernel, out_shape=out_shape, in_specs=in_specs or [VMEM] *...]
    add x27 -> x0, local copies, waits for them, and re-layouts: 79.4 us -> none  [the longest x18 74.4 us: sliced(): return jnp.floor(code_table / step_size) * step_size + step_size / 2.0]
    unnamed x1 -> x0, blocking collectives: 67.2 us -> none
    ppermute x4 -> x35, starting transfers between devices: 20 us -> 75.7 us  [the longest x24 62.2 us: send(): return lax.ppermute(a, AX, stage_pairs(stage, r % 4))]
    unnamed x464 -> x83, local copies, waits for them, and re-layouts: 66.6 us -> 12 us
  transfers between devices with their start and end apart: 6 -> 35, of which waited for: 2 -> 21; matrix products, arithmetic and copies ran while one was open for 17% -> 3% of each run, Pallas kernels for 0% -> 18%
where the time goes in v1:
time: 245 us; the launch traced here: 240 us
  Pallas kernels  94.6 us (39%)
  starting transfers between devices  75.7 us (31%)
  waiting for transfers between devices  49.2 us (20%)
  local copies, waits for them, and re-layouts  14.6 us (6%)
  other arithmetic  4.78 us (2%)
    ppermute x24, starting transfers between devices, send(): return lax.ppermute(a, AX, stage_pairs(stage, r % 4))  62.2 us
    pallas_call x11, Pallas kernels, call(): pl.pallas_call(kernel, out_shape=out_shape, in_specs=in_specs or [VMEM] *...  50.5 us
    pallas_call x1, Pallas kernels, run_middle(): pl.pallas_call(middle_kernel, out_shape=out_shape, in_specs=[SMEM, SMEM]...  41.9 us
    ppermute x24, waiting for transfers between devices, send(): return lax.ppermute(a, AX, stage_pairs(stage, r % 4))  39.3 us
    unnamed x83, local copies, waits for them, and re-layouts  12 us
    ppermute x7, waiting for transfers between devices, other_core(): return lax.ppermute(a, 'c', [(0, 1), (1, 0)])  9.36 us
    ppermute x2, starting transfers between devices, gather(): t1, t0 = (lax.ppermute(tokens, ('y', 'x'), behind(k)) for k in (1, 2))  7.62 us
  transfers between devices with their start and end apart: 35, of which 21 were waited for; matrix products, arithmetic and copies ran while one was open for 3% of the time, Pallas kernels for 18%

profile of v1, /device:TPU:8, one launch (start us, length us, event | category | flops | bytes accessed | tf_op | source)
XLA Modules:
  0.0 240.4 jit_solution(1022560634782652209)
XLA Ops:
  3.6 2.8 %collective-permute-start.2 = (bf16[352,128]{1,0:T(8,128)(2,1)}, bf16[352,128]{1,0:T(8,128)(2,1)S(1)}, u32[]{:S(2)}, u32[]{:S(2)}) collective-permute-start(bf16[352,128]{1,0:T(8,128)(2,1)} %pack.1), channel_id=1, source_target_pairs={{0,3},{1,0},{2,1},{3,2},{4,7},{5,4},{6,5},{7,6},{8,11},{9,8},{10,9... | collective-permute-start | bytes 270344 | tf_op jit(solution)/shard_map/ppermute | solution.py:103
  8.1 3.7 %collective-permute-start.4 = (bf16[256,640]{1,0:T(8,128)(2,1)}, bf16[256,640]{1,0:T(8,128)(2,1)S(1)}, u32[]{:S(2)}, u32[]{:S(2)}) collective-permute-start(bf16[256,640]{1,0:T(8,128)(2,1)} %tok.3), channel_id=1, source_target_pairs={{0,1},{1,2},{2,3},{3,4},{4,5},{5,6},{6,7},{8,9},{9,10},{10,11},{11... | collective-permute-start | bytes 983048 | tf_op jit(solution)/shard_map/ppermute | solution.py:148
  11.8 3.9 %collective-permute-start.3 = (bf16[256,640]{1,0:T(8,128)(2,1)}, bf16[256,640]{1,0:T(8,128)(2,1)S(1)}, u32[]{:S(2)}, u32[]{:S(2)}) collective-permute-start(bf16[256,640]{1,0:T(8,128)(2,1)} %tok.3), channel_id=1, source_target_pairs={{0,2},{1,3},{2,4},{3,5},{4,6},{5,7},{8,10},{9,11},{10,12},{11,13},... | collective-permute-start | bytes 983048 | tf_op jit(solution)/shard_map/ppermute | solution.py:148
  19.3 2.6 %collective-permute-start.6 = (bf16[1408,128]{1,0:T(8,128)(2,1)S(1)}, bf16[1408,128]{1,0:T(8,128)(2,1)S(1)}, u32[]{:S(2)}, u32[]{:S(2)}) collective-permute-start(bf16[1408,128]{1,0:T(8,128)(2,1)S(1)} %pad_maximum_fusion.refs_0_), channel_id=1, source_target_pairs={{0,8},{1,9},{2,10},{3,11},{4,12},{5,13},{6,14},{7,15},{8,0},{9,1},... | collective-permute-start | bytes 1081352 | tf_op jit(solution)/shard_map/ppermute | solution.py:103
  25.5 2.5 %multiply_sine_fusion = (f32[768,128]{1,0:T(8,128)}, f32[768,128]{1,0:T(8,128)}) fusion(f32[128]{0:T(128)S(1)} %multiply_power_fusion, f32[768]{0:T(1024)S(1)} %add_convert_fusion), kind=kLoop, calls=%fused_computation | loop fusion | flops 98304 | bytes 790016 | tf_op jit(solution)/shard_map/sin | solution.py:870
  28.5 2.6 %collective-permute-done.6.refs_2_ = bf16[1408,128]{1,0:T(8,128)(2,1)S(1)} collective-permute-done((bf16[1408,128]{1,0:T(8,128)(2,1)S(1)}, bf16[1408,128]{1,0:T(8,128)(2,1)S(1)}, u32[]{:S(2)}, u32[]{:S(2)}) %collective-permute-start.6) | collective-permute-done | bytes 360480 | tf_op jit(solution)/shard_map/ppermute | solution.py:103
  31.1 5.2 %collective-permute-done.5.refs_1_ = bf16[1408,128]{1,0:T(8,128)(2,1)} collective-permute-done((bf16[1408,128]{1,0:T(8,128)(2,1)S(1)}, bf16[1408,128]{1,0:T(8,128)(2,1)}, u32[]{:S(2)}, u32[]{:S(2)}) %collective-permute-start.5) | collective-permute-done | bytes 360480 | tf_op jit(solution)/shard_map/ppermute | solution.py:103
  36.3 3.0 %asm.1 = (bf16[1024,128]{1,0:T(8,128)(2,1)}, bf16[4608,128]{1,0:T(8,128)(2,1)}) custom-call(bf16[1408,128]{1,0:T(8,128)(2,1)} %copy-done.31, bf16[1408,128]{1,0:T(8,128)(2,1)} %collective-permute-done.5.refs_1_, bf16[1408,128]{1,0:T(8,128)(2,1)} %copy-done.36, bf16[1408,128]{1,0:T(8,128)(2,1)} %copy-done.35), custom_call_target="tpu_custom_call" | custom-call | flops 1000 | bytes 1000 | tf_op jit(solution)/shard_map/asm/pallas_call | solution.py:59
  39.3 4.0 %collective-permute-start.10 = (bf16[1024,128]{1,0:T(8,128)(2,1)}, bf16[1024,128]{1,0:T(8,128)(2,1)S(1)}, u32[]{:S(2)}, u32[]{:S(2)}) collective-permute-start(bf16[1024,128]{1,0:T(8,128)(2,1)} %get-tuple-element.95.a), channel_id=1, source_target_pairs={{0,80},{1,81},{2,82},{3,83},{4,84},{5,85},{6,86},{7,87},{8,88},{9,... | collective-permute-start | bytes 786440 | tf_op jit(solution)/shard_map/ppermute | solution.py:103
  44.6 2.0 collective-permute-start.14
  46.6 2.3 collective-permute-start.13
  51.5 2.4 %collective-permute-done.8.b = bf16[1024,128]{1,0:T(8,128)(2,1)S(1)} collective-permute-done((bf16[1024,128]{1,0:T(8,128)(2,1)}, bf16[1024,128]{1,0:T(8,128)(2,1)S(1)}, u32[]{:S(2)}, u32[]{:S(2)}) %collective-permute-start.8) | collective-permute-done | bytes 262176 | tf_op jit(solution)/shard_map/ppermute | solution.py:103
  54.6 2.2 join.1.mine
  60.8 16.5 %first.1 = (f32[1,9472]{1,0:T(1,128)}, bf16[768,640]{1,0:T(8,128)(2,1)}, bf16[3,2,512,256]{3,2,1,0:T(8,128)(2,1)}, bf16[3,768,512]{2,1,0:T(8,128)(2,1)}, bf16[3,256,1024]{2,1,0:T(8,128)(2,1)}) custom-call(s32[3]{0:T(128)} %fusion.30.run, bf16[4096,128]{1,0:T(8,128)(2,1)} %join.1.mine, bf16[4096,128]{1,0:T(8,128)(2,1)} %copy-done.12, ...), custom_call_target="tpu_custom_call" | custom-call | flops 20001000 | bytes 1000 | tf_op jit(solution)/shard_map/first/pallas_call | solution.py:59
  77.3 2.3 collective-permute-done.12.b1
  80.7 2.0 collective-permute-done.16.b5
  87.1 41.9 %middle.1 = (f32[3,256,640]{2,1,0:T(8,128)}, f32[256,640]{1,0:T(8,128)}, bf16[3,256,1024]{2,1,0:T(8,128)(2,1)}, bf16[18432,128]{1,0:T(8,128)(2,1)}, bf16[18432,128]{1,0:T(8,128)(2,1)}, /*index=5*/f32[1,9472]{1,0:T(1,128)}) custom-call(s32[3]{0:T(128)} %fusion.30.run, s32[128]{0:T(128)} %get-tuple-element.93.inat, ...), custom_call_target="tpu_custom_call" | custom-call | flops 70001000 | bytes 1000 | tf_op jit(solution)/shard_map/middle/pallas_call | solution.py:787
  135.8 7.5 %attnb0.1 = (bf16[1,256,1024]{2,1,0:T(8,128)(2,1)S(1)}, bf16[1,768,512]{2,1,0:T(8,128)(2,1)S(1)}, f32[1,9472]{1,0:T(1,128)S(1)}) custom-call(s32[3]{0:T(128)S(1)} %copy-done.30, f32[1,9472]{1,0:T(1,128)S(1)} %copy-done.21, f32[768,128]{1,0:T(8,128)S(1)} %copy-done.8, f32[768,128]{1,0:T(8,128)S(1)} %copy-done.7, s32[256,1]{1,0:T(8,128)S(1)} %copy-done.14, ...), custom_call_target="tpu_custom_call" | custom-call | flops 8001000 | bytes 1000 | tf_op jit(solution)/shard_map/attnb0/pallas_call | solution.py:59
  143.4 2.0 rs1_4608.1
  145.4 15.7 %collective-permute-start.23 = (bf16[4608,128]{1,0:T(8,128)(2,1)S(1)}, bf16[4608,128]{1,0:T(8,128)(2,1)S(1)}, u32[]{:S(2)}, u32[]{:S(2)}) collective-permute-start(bf16[4608,128]{1,0:T(8,128)(2,1)S(1)} %get-tuple-element.137), channel_id=1, source_target_pairs={{0,16},{1,17},{2,18},{3,19},{4,20},{5,21},{6,22},{7,23},{8,24},{9,... | collective-permute-start | bytes 3538952 | tf_op jit(solution)/shard_map/ppermute | solution.py:103
  162.6 7.5 %attnb1.1 = (bf16[2,256,1024]{2,1,0:T(8,128)(2,1)S(1)}, bf16[2,768,512]{2,1,0:T(8,128)(2,1)S(1)}, f32[1,9472]{1,0:T(1,128)S(1)}) custom-call(s32[3]{0:T(128)S(1)} %copy-done.30, f32[1,9472]{1,0:T(1,128)S(1)} %copy-done.22, f32[768,128]{1,0:T(8,128)S(1)} %copy-done.9, f32[768,128]{1,0:T(8,128)S(1)} %copy-done.7, s32[256,1]{1,0:T(8,128)S(1)} %copy-done.15, ...), custom_call_target="tpu_custom_call" | custom-call | flops 16001000 | bytes 1000 | tf_op jit(solution)/shard_map/attnb1/pallas_call | solution.py:59
  170.2 9.0 %last.1 = (f32[256,640]{1,0:T(8,128)S(1)}, bf16[256,640]{1,0:T(8,128)(2,1)S(1)}, bf16[256,640]{1,0:T(8,128)(2,1)S(1)}, bf16[4096,128]{1,0:T(8,128)(2,1)S(1)}, bf16[4096,128]{1,0:T(8,128)(2,1)S(1)}) custom-call(s32[3]{0:T(128)S(1)} %copy-done.30, bf16[768,640]{1,0:T(8,128)(2,1)S(1)} %copy-done.20, bf16[4096,128]{1,0:T(8,128)(2,1)S(1)} %copy-done.3, ...), custom_call_target="tpu_custom_call" | custom-call | flops 14001000 | bytes 1000 | tf_op jit(solution)/shard_map/last/pallas_call | solution.py:59
  179.3 8.7 %collective-permute-done.24.refs_7_ = bf16[4608,128]{1,0:T(8,128)(2,1)S(1)} collective-permute-done((bf16[4608,128]{1,0:T(8,128)(2,1)S(1)}, bf16[4608,128]{1,0:T(8,128)(2,1)S(1)}, u32[]{:S(2)}, u32[]{:S(2)}) %collective-permute-start.24) | collective-permute-done | bytes 1179680 | tf_op jit(solution)/shard_map/ppermute | solution.py:103
  188.0 2.7 %collective-permute-done.25 = bf16[4096,128]{1,0:T(8,128)(2,1)S(1)} collective-permute-done((bf16[4096,128]{1,0:T(8,128)(2,1)S(1)}, bf16[4096,128]{1,0:T(8,128)(2,1)S(1)}, u32[]{:S(2)}, u32[]{:S(2)}) %collective-permute-start.25) | collective-permute-done | bytes 1048608 | tf_op jit(solution)/shard_map/ppermute | solution.py:111
  191.6 3.5 %collective-permute-start.27 = (bf16[1024,128]{1,0:T(8,128)(2,1)S(1)}, bf16[1024,128]{1,0:T(8,128)(2,1)S(1)}, u32[]{:S(2)}, u32[]{:S(2)}) collective-permute-start(bf16[1024,128]{1,0:T(8,128)(2,1)S(1)} %get-tuple-element.142), channel_id=1, source_target_pairs={{0,16},{1,17},{2,18},{3,19},{4,20},{5,21},{6,22},{7,23},{8,24},{9,... | collective-permute-start | bytes 786440 | tf_op jit(solution)/shard_map/ppermute | solution.py:103
  197.4 2.1 collective-permute-done.27.refs_2_
  199.4 3.2 %collective-permute-done.28.refs_3_ = bf16[1024,128]{1,0:T(8,128)(2,1)S(1)} collective-permute-done((bf16[1024,128]{1,0:T(8,128)(2,1)S(1)}, bf16[1024,128]{1,0:T(8,128)(2,1)S(1)}, u32[]{:S(2)}, u32[]{:S(2)}) %collective-permute-start.28) | collective-permute-done | bytes 262176 | tf_op jit(solution)/shard_map/ppermute | solution.py:103
  203.7 3.5 %collective-permute-start.30 = (bf16[1408,128]{1,0:T(8,128)(2,1)S(1)}, bf16[1408,128]{1,0:T(8,128)(2,1)S(1)}, u32[]{:S(2)}, u32[]{:S(2)}) collective-permute-start(bf16[1408,128]{1,0:T(8,128)(2,1)S(1)} %get-tuple-element.150), channel_id=1, source_target_pairs={{0,8},{1,9},{2,10},{3,11},{4,12},{5,13},{6,14},{7,15},{8,0},{9,1},... | collective-permute-start | bytes 1081352 | tf_op jit(solution)/shard_map/ppermute | solution.py:103
  207.3 2.5 %collective-permute-start.31 = (bf16[1408,128]{1,0:T(8,128)(2,1)S(1)}, bf16[1408,128]{1,0:T(8,128)(2,1)S(1)}, u32[]{:S(2)}, u32[]{:S(2)}) collective-permute-start(bf16[1408,128]{1,0:T(8,128)(2,1)S(1)} %get-tuple-element.151), channel_id=1, source_target_pairs={{0,4},{1,5},{2,6},{3,7},{4,8},{5,9},{6,10},{7,11},{8,12},{9,13},{1... | collective-permute-start | bytes 1081352 | tf_op jit(solution)/shard_map/ppermute | solution.py:103
  213.7 2.8 %collective-permute-done.30.refs_2_ = bf16[1408,128]{1,0:T(8,128)(2,1)S(1)} collective-permute-done((bf16[1408,128]{1,0:T(8,128)(2,1)S(1)}, bf16[1408,128]{1,0:T(8,128)(2,1)S(1)}, u32[]{:S(2)}, u32[]{:S(2)}) %collective-permute-start.30) | collective-permute-done | bytes 360480 | tf_op jit(solution)/shard_map/ppermute | solution.py:103
  217.8 14.1 %collective-permute-start.32 = (bf16[352,128]{1,0:T(8,128)(2,1)S(1)}, bf16[352,128]{1,0:T(8,128)(2,1)S(1)}, u32[]{:S(2)}, u32[]{:S(2)}) collective-permute-start(bf16[352,128]{1,0:T(8,128)(2,1)S(1)} %get-tuple-element.153), channel_id=1, source_target_pairs={{0,3},{1,0},{2,1},{3,2},{4,7},{5,4},{6,5},{7,6},{8,11},{9,8},{10,9... | collective-permute-start | bytes 270344 | tf_op jit(solution)/shard_map/ppermute | solution.py:103
  234.9 3.1 %collective-permute-done.33.a2 = bf16[352,128]{1,0:T(8,128)(2,1)S(1)} collective-permute-done((bf16[352,128]{1,0:T(8,128)(2,1)S(1)}, bf16[352,128]{1,0:T(8,128)(2,1)S(1)}, u32[]{:S(2)}, u32[]{:S(2)}) %collective-permute-start.33) | collective-permute-done | bytes 90144 | tf_op jit(solution)/shard_map/ppermute | solution.py:103
  (147 shorter events, 48.9 us)
Async XLA Ops:
  3.6 14.1 %collective-permute-start.2 = (bf16[352,128]{1,0:T(8,128)(2,1)}, bf16[352,128]{1,0:T(8,128)(2,1)S(1)}, u32[]{:S(2)}, u32[]{:S(2)}) collective-permute-start(bf16[352,128]{1,0:T(8,128)(2,1)} %pack.1), channel_id=1, source_target_pairs={{0,3},{1,0},{2,1},{3,2},{4,7},{5,4},{6,5},{7,6},{8,11},{9,8},{10,9... | collective-permute-start | bytes 270344 | tf_op jit(solution)/shard_map/ppermute | solution.py:103
  6.4 11.4 %collective-permute-start.1 = (bf16[352,128]{1,0:T(8,128)(2,1)}, bf16[352,128]{1,0:T(8,128)(2,1)S(1)}, u32[]{:S(2)}, u32[]{:S(2)}) collective-permute-start(bf16[352,128]{1,0:T(8,128)(2,1)} %pack.1), channel_id=1, source_target_pairs={{0,2},{1,3},{2,0},{3,1},{4,6},{5,7},{6,4},{7,5},{8,10},{9,11},{10,... | collective-permute-start | bytes 270344 | tf_op jit(solution)/shard_map/ppermute | solution.py:103
  7.2 10.6 %collective-permute-start = (bf16[352,128]{1,0:T(8,128)(2,1)}, bf16[352,128]{1,0:T(8,128)(2,1)S(1)}, u32[]{:S(2)}, u32[]{:S(2)}) collective-permute-start(bf16[352,128]{1,0:T(8,128)(2,1)} %pack.1), channel_id=1, source_target_pairs={{0,1},{1,2},{2,3},{3,0},{4,5},{5,6},{6,7},{7,4},{8,9},{9,10},{10,1... | collective-permute-start | bytes 270344 | tf_op jit(solution)/shard_map/ppermute | solution.py:103
  8.1 20.4 %collective-permute-start.4 = (bf16[256,640]{1,0:T(8,128)(2,1)}, bf16[256,640]{1,0:T(8,128)(2,1)S(1)}, u32[]{:S(2)}, u32[]{:S(2)}) collective-permute-start(bf16[256,640]{1,0:T(8,128)(2,1)} %tok.3), channel_id=1, source_target_pairs={{0,1},{1,2},{2,3},{3,4},{4,5},{5,6},{6,7},{8,9},{9,10},{10,11},{11... | collective-permute-start | bytes 983048 | tf_op jit(solution)/shard_map/ppermute | solution.py:148
  11.8 16.7 %collective-permute-start.3 = (bf16[256,640]{1,0:T(8,128)(2,1)}, bf16[256,640]{1,0:T(8,128)(2,1)S(1)}, u32[]{:S(2)}, u32[]{:S(2)}) collective-permute-start(bf16[256,640]{1,0:T(8,128)(2,1)} %tok.3), channel_id=1, source_target_pairs={{0,2},{1,3},{2,4},{3,5},{4,6},{5,7},{8,10},{9,11},{10,12},{11,13},... | collective-permute-start | bytes 983048 | tf_op jit(solution)/shard_map/ppermute | solution.py:148
  18.7 9.8 %collective-permute-start.7 = (bf16[1408,128]{1,0:T(8,128)(2,1)S(1)}, bf16[1408,128]{1,0:T(8,128)(2,1)S(1)}, u32[]{:S(2)}, u32[]{:S(2)}) collective-permute-start(bf16[1408,128]{1,0:T(8,128)(2,1)S(1)} %pad_maximum_fusion.refs_0_), channel_id=1, source_target_pairs={{0,12},{1,13},{2,14},{3,15},{4,0},{5,1},{6,2},{7,3},{8,4},{9,5},{1... | collective-permute-start | bytes 1081352 | tf_op jit(solution)/shard_map/ppermute | solution.py:103
  19.3 11.9 %collective-permute-start.6 = (bf16[1408,128]{1,0:T(8,128)(2,1)S(1)}, bf16[1408,128]{1,0:T(8,128)(2,1)S(1)}, u32[]{:S(2)}, u32[]{:S(2)}) collective-permute-start(bf16[1408,128]{1,0:T(8,128)(2,1)S(1)} %pad_maximum_fusion.refs_0_), channel_id=1, source_target_pairs={{0,8},{1,9},{2,10},{3,11},{4,12},{5,13},{6,14},{7,15},{8,0},{9,1},... | collective-permute-start | bytes 1081352 | tf_op jit(solution)/shard_map/ppermute | solution.py:103
  21.8 14.4 %collective-permute-start.5 = (bf16[1408,128]{1,0:T(8,128)(2,1)S(1)}, bf16[1408,128]{1,0:T(8,128)(2,1)}, u32[]{:S(2)}, u32[]{:S(2)}) collective-permute-start(bf16[1408,128]{1,0:T(8,128)(2,1)S(1)} %pad_maximum_fusion.refs_0_), channel_id=1, source_target_pairs={{0,4},{1,5},{2,6},{3,7},{4,8},{5,9},{6,10},{7,11},{8,12},{9,13},{1... | collective-permute-start | bytes 1081352 | tf_op jit(solution)/shard_map/ppermute | solution.py:103
  39.3 11.0 %collective-permute-start.10 = (bf16[1024,128]{1,0:T(8,128)(2,1)}, bf16[1024,128]{1,0:T(8,128)(2,1)S(1)}, u32[]{:S(2)}, u32[]{:S(2)}) collective-permute-start(bf16[1024,128]{1,0:T(8,128)(2,1)} %get-tuple-element.95.a), channel_id=1, source_target_pairs={{0,80},{1,81},{2,82},{3,83},{4,84},{5,85},{6,86},{7,87},{8,88},{9,... | collective-permute-start | bytes 786440 | tf_op jit(solution)/shard_map/ppermute | solution.py:103
  43.3 8.2 %collective-permute-start.9 = (bf16[1024,128]{1,0:T(8,128)(2,1)}, bf16[1024,128]{1,0:T(8,128)(2,1)S(1)}, u32[]{:S(2)}, u32[]{:S(2)}) collective-permute-start(bf16[1024,128]{1,0:T(8,128)(2,1)} %get-tuple-element.95.a), channel_id=1, source_target_pairs={{0,16},{1,17},{2,18},{3,19},{4,20},{5,21},{6,22},{7,23},{8,24},{9,... | collective-permute-start | bytes 786440 | tf_op jit(solution)/shard_map/ppermute | solution.py:103
  43.3 10.6 %collective-permute-start.8 = (bf16[1024,128]{1,0:T(8,128)(2,1)}, bf16[1024,128]{1,0:T(8,128)(2,1)S(1)}, u32[]{:S(2)}, u32[]{:S(2)}) collective-permute-start(bf16[1024,128]{1,0:T(8,128)(2,1)} %get-tuple-element.95.a), channel_id=1, source_target_pairs={{0,64},{1,65},{2,66},{3,67},{4,68},{5,69},{6,70},{7,71},{8,72},{9,... | collective-permute-start | bytes 786440 | tf_op jit(solution)/shard_map/ppermute | solution.py:103
  44.6 32.7 %collective-permute-start.14 = (bf16[4608,128]{1,0:T(8,128)(2,1)}, bf16[4608,128]{1,0:T(8,128)(2,1)}, u32[]{:S(2)}, u32[]{:S(2)}) collective-permute-start(bf16[4608,128]{1,0:T(8,128)(2,1)} %get-tuple-element.105.b0), channel_id=1, source_target_pairs={{0,80},{1,81},{2,82},{3,83},{4,84},{5,85},{6,86},{7,87},{8,88},{9,... | collective-permute-start | bytes 3538952 | tf_op jit(solution)/shard_map/ppermute | solution.py:103
  46.6 30.7 %collective-permute-start.13 = (bf16[4608,128]{1,0:T(8,128)(2,1)}, bf16[4608,128]{1,0:T(8,128)(2,1)}, u32[]{:S(2)}, u32[]{:S(2)}) collective-permute-start(bf16[4608,128]{1,0:T(8,128)(2,1)} %get-tuple-element.105.b0), channel_id=1, source_target_pairs={{0,16},{1,17},{2,18},{3,19},{4,20},{5,21},{6,22},{7,23},{8,24},{9,... | collective-permute-start | bytes 3538952 | tf_op jit(solution)/shard_map/ppermute | solution.py:103
  50.3 29.3 %collective-permute-start.12 = (bf16[4608,128]{1,0:T(8,128)(2,1)}, bf16[4608,128]{1,0:T(8,128)(2,1)}, u32[]{:S(2)}, u32[]{:S(2)}) collective-permute-start(bf16[4608,128]{1,0:T(8,128)(2,1)} %get-tuple-element.105.b0), channel_id=1, source_target_pairs={{0,64},{1,65},{2,66},{3,67},{4,68},{5,69},{6,70},{7,71},{8,72},{9,... | collective-permute-start | bytes 3538952 | tf_op jit(solution)/shard_map/ppermute | solution.py:103
  57.7 23.0 %collective-permute-start.15 = (bf16[4608,128]{1,0:T(8,128)(2,1)}, bf16[4608,128]{1,0:T(8,128)(2,1)}, u32[]{:S(2)}, u32[]{:S(2)}) collective-permute-start(bf16[4608,128]{1,0:T(8,128)(2,1)} %get-tuple-element.105.b0), channel_id=1, source_target_pairs={{0,32},{32,0},{1,33},{33,1},{2,34},{34,2},{3,35},{35,3},{4,36},{36... | collective-permute-start | bytes 3538952 | tf_op jit(solution)/shard_map/ppermute | solution.py:111
  79.6 4.7 %collective-permute-start.17 = (bf16[4608,128]{1,0:T(8,128)(2,1)}, bf16[4608,128]{1,0:T(8,128)(2,1)S(1)}, u32[]{:S(2)}, u32[]{:S(2)}) collective-permute-start(bf16[4608,128]{1,0:T(8,128)(2,1)} %collective-permute-done.13.b2), channel_id=1, source_target_pairs={{0,32},{32,0},{1,33},{33,1},{2,34},{34,2},{3,35},{35,3},{4,36},{36... | collective-permute-start | bytes 3538952 | tf_op jit(solution)/shard_map/ppermute | solution.py:111
  80.2 5.9 %collective-permute-start.18 = (bf16[4608,128]{1,0:T(8,128)(2,1)}, bf16[4608,128]{1,0:T(8,128)(2,1)S(1)}, u32[]{:S(2)}, u32[]{:S(2)}) collective-permute-start(bf16[4608,128]{1,0:T(8,128)(2,1)} %collective-permute-done.14.b3), channel_id=1, source_target_pairs={{0,32},{32,0},{1,33},{33,1},{2,34},{34,2},{3,35},{35,3},{4,36},{36... | collective-permute-start | bytes 3538952 | tf_op jit(solution)/shard_map/ppermute | solution.py:111
  129.0 14.3 %collective-permute-start.19 = (bf16[18432,128]{1,0:T(8,128)(2,1)}, bf16[18432,128]{1,0:T(8,128)(2,1)S(1)}, u32[]{:S(2)}, u32[]{:S(2)}) collective-permute-start(bf16[18432,128]{1,0:T(8,128)(2,1)} %get-tuple-element.120), channel_id=1, source_target_pairs={{0,32},{32,0},{1,33},{33,1},{2,34},{34,2},{3,35},{35,3},{4,36},{36... | collective-permute-start | bytes 14155784 | tf_op jit(solution)/shard_map/ppermute | solution.py:111
  145.3 33.9 %collective-permute-start.22 = (bf16[4608,128]{1,0:T(8,128)(2,1)S(1)}, bf16[4608,128]{1,0:T(8,128)(2,1)S(1)}, u32[]{:S(2)}, u32[]{:S(2)}) collective-permute-start(bf16[4608,128]{1,0:T(8,128)(2,1)S(1)} %get-tuple-element.136), channel_id=1, source_target_pairs={{0,80},{1,81},{2,82},{3,83},{4,84},{5,85},{6,86},{7,87},{8,88},{9,... | collective-permute-start | bytes 3538952 | tf_op jit(solution)/shard_map/ppermute | solution.py:103
  145.4 33.8 %collective-permute-start.23 = (bf16[4608,128]{1,0:T(8,128)(2,1)S(1)}, bf16[4608,128]{1,0:T(8,128)(2,1)S(1)}, u32[]{:S(2)}, u32[]{:S(2)}) collective-permute-start(bf16[4608,128]{1,0:T(8,128)(2,1)S(1)} %get-tuple-element.137), channel_id=1, source_target_pairs={{0,16},{1,17},{2,18},{3,19},{4,20},{5,21},{6,22},{7,23},{8,24},{9,... | collective-permute-start | bytes 3538952 | tf_op jit(solution)/shard_map/ppermute | solution.py:103
  161.2 26.8 %collective-permute-start.24 = (bf16[4608,128]{1,0:T(8,128)(2,1)S(1)}, bf16[4608,128]{1,0:T(8,128)(2,1)S(1)}, u32[]{:S(2)}, u32[]{:S(2)}) collective-permute-start(bf16[4608,128]{1,0:T(8,128)(2,1)S(1)} %get-tuple-element.138), channel_id=1, source_target_pairs={{0,64},{1,65},{2,66},{3,67},{4,68},{5,69},{6,70},{7,71},{8,72},{9,... | collective-permute-start | bytes 3538952 | tf_op jit(solution)/shard_map/ppermute | solution.py:103
  190.9 6.5 %collective-permute-start.26 = (bf16[1024,128]{1,0:T(8,128)(2,1)S(1)}, bf16[1024,128]{1,0:T(8,128)(2,1)S(1)}, u32[]{:S(2)}, u32[]{:S(2)}) collective-permute-start(bf16[1024,128]{1,0:T(8,128)(2,1)S(1)} %get-tuple-element.141), channel_id=1, source_target_pairs={{0,80},{1,81},{2,82},{3,83},{4,84},{5,85},{6,86},{7,87},{8,88},{9,... | collective-permute-start | bytes 786440 | tf_op jit(solution)/shard_map/ppermute | solution.py:103
  191.6 7.9 %collective-permute-start.27 = (bf16[1024,128]{1,0:T(8,128)(2,1)S(1)}, bf16[1024,128]{1,0:T(8,128)(2,1)S(1)}, u32[]{:S(2)}, u32[]{:S(2)}) collective-permute-start(bf16[1024,128]{1,0:T(8,128)(2,1)S(1)} %get-tuple-element.142), channel_id=1, source_target_pairs={{0,16},{1,17},{2,18},{3,19},{4,20},{5,21},{6,22},{7,23},{8,24},{9,... | collective-permute-start | bytes 786440 | tf_op jit(solution)/shard_map/ppermute | solution.py:103
  195.1 7.6 %collective-permute-start.28 = (bf16[1024,128]{1,0:T(8,128)(2,1)S(1)}, bf16[1024,128]{1,0:T(8,128)(2,1)S(1)}, u32[]{:S(2)}, u32[]{:S(2)}) collective-permute-start(bf16[1024,128]{1,0:T(8,128)(2,1)S(1)} %get-tuple-element.143), channel_id=1, source_target_pairs={{0,64},{1,65},{2,66},{3,67},{4,68},{5,69},{6,70},{7,71},{8,72},{9,... | collective-permute-start | bytes 786440 | tf_op jit(solution)/shard_map/ppermute | solution.py:103
  203.6 10.0 %collective-permute-start.29 = (bf16[1408,128]{1,0:T(8,128)(2,1)S(1)}, bf16[1408,128]{1,0:T(8,128)(2,1)S(1)}, u32[]{:S(2)}, u32[]{:S(2)}) collective-permute-start(bf16[1408,128]{1,0:T(8,128)(2,1)S(1)} %get-tuple-element.149), channel_id=1, source_target_pairs={{0,12},{1,13},{2,14},{3,15},{4,0},{5,1},{6,2},{7,3},{8,4},{9,5},{1... | collective-permute-start | bytes 1081352 | tf_op jit(solution)/shard_map/ppermute | solution.py:103
  203.7 12.7 %collective-permute-start.30 = (bf16[1408,128]{1,0:T(8,128)(2,1)S(1)}, bf16[1408,128]{1,0:T(8,128)(2,1)S(1)}, u32[]{:S(2)}, u32[]{:S(2)}) collective-permute-start(bf16[1408,128]{1,0:T(8,128)(2,1)S(1)} %get-tuple-element.150), channel_id=1, source_target_pairs={{0,8},{1,9},{2,10},{3,11},{4,12},{5,13},{6,14},{7,15},{8,0},{9,1},... | collective-permute-start | bytes 1081352 | tf_op jit(solution)/shard_map/ppermute | solution.py:103
  207.3 10.4 %collective-permute-start.31 = (bf16[1408,128]{1,0:T(8,128)(2,1)S(1)}, bf16[1408,128]{1,0:T(8,128)(2,1)S(1)}, u32[]{:S(2)}, u32[]{:S(2)}) collective-permute-start(bf16[1408,128]{1,0:T(8,128)(2,1)S(1)} %get-tuple-element.151), channel_id=1, source_target_pairs={{0,4},{1,5},{2,6},{3,7},{4,8},{5,9},{6,10},{7,11},{8,12},{9,13},{1... | collective-permute-start | bytes 1081352 | tf_op jit(solution)/shard_map/ppermute | solution.py:103
  209.8 23.0 %collective-permute-start.20 = (bf16[256,640]{1,0:T(8,128)(2,1)S(1)}, bf16[256,640]{1,0:T(8,128)(2,1)S(1)}, u32[]{:S(2)}, u32[]{:S(2)}) collective-permute-start(bf16[256,640]{1,0:T(8,128)(2,1)S(1)} %get-tuple-element.130), channel_id=1, source_target_pairs={{1,0},{2,1},{3,2},{4,3},{5,4},{6,5},{7,6},{9,8},{10,9},{11,10},{12... | collective-permute-start | bytes 983048 | tf_op jit(solution)/shard_map/ppermute | solution.py:907
  211.7 21.1 %collective-permute-start.21 = (bf16[256,640]{1,0:T(8,128)(2,1)S(1)}, bf16[256,640]{1,0:T(8,128)(2,1)S(1)}, u32[]{:S(2)}, u32[]{:S(2)}) collective-permute-start(bf16[256,640]{1,0:T(8,128)(2,1)S(1)} %get-tuple-element.131), channel_id=1, source_target_pairs={{2,0},{3,1},{4,2},{5,3},{6,4},{7,5},{10,8},{11,9},{12,10},{13,11},... | collective-permute-start | bytes 983048 | tf_op jit(solution)/shard_map/ppermute | solution.py:908
  217.8 17.1 %collective-permute-start.32 = (bf16[352,128]{1,0:T(8,128)(2,1)S(1)}, bf16[352,128]{1,0:T(8,128)(2,1)S(1)}, u32[]{:S(2)}, u32[]{:S(2)}) collective-permute-start(bf16[352,128]{1,0:T(8,128)(2,1)S(1)} %get-tuple-element.153), channel_id=1, source_target_pairs={{0,3},{1,0},{2,1},{3,2},{4,7},{5,4},{6,5},{7,6},{8,11},{9,8},{10,9... | collective-permute-start | bytes 270344 | tf_op jit(solution)/shard_map/ppermute | solution.py:103
  231.9 6.1 %collective-permute-start.33 = (bf16[352,128]{1,0:T(8,128)(2,1)S(1)}, bf16[352,128]{1,0:T(8,128)(2,1)S(1)}, u32[]{:S(2)}, u32[]{:S(2)}) collective-permute-start(bf16[352,128]{1,0:T(8,128)(2,1)S(1)} %get-tuple-element.154), channel_id=1, source_target_pairs={{0,2},{1,3},{2,0},{3,1},{4,6},{5,7},{6,4},{7,5},{8,10},{9,11},{10,... | collective-permute-start | bytes 270344 | tf_op jit(solution)/shard_map/ppermute | solution.py:103
  231.9 6.7 %collective-permute-start.34 = (bf16[352,128]{1,0:T(8,128)(2,1)S(1)}, bf16[352,128]{1,0:T(8,128)(2,1)S(1)}, u32[]{:S(2)}, u32[]{:S(2)}) collective-permute-start(bf16[352,128]{1,0:T(8,128)(2,1)S(1)} %get-tuple-element.155), channel_id=1, source_target_pairs={{0,1},{1,2},{2,3},{3,0},{4,5},{5,6},{6,7},{7,4},{8,9},{9,10},{10,1... | collective-permute-start | bytes 270344 | tf_op jit(solution)/shard_map/ppermute | solution.py:103
  (43 other events, 510.1 us)

commit v2 on v1

--- a/solution.py
+++ b/solution.py
@@ -45,7 +45,7 @@
     for g in range(4):
         c = np.arange(D)
         at = ON + g * D
-        lane[0, at : at + D] = 54 + (c % 5) * 4 + g
+        lane[0, at : at + D] = 54 + g * 5 + c % 5
         dev[0, at : at + D] = c // 5
     return lane, dev
 
@@ -163,13 +163,17 @@
 
 def total4(refs, at, rows):
     t = refs[0][at : at + rows, :].astype(F32)
-    for k in (1, 2, 3):
-        t = t + refs[k][at : at + rows, :].astype(F32)
+    for ref in refs[1:]:
+        t = t + ref[at : at + rows, :].astype(F32)
     return t
 
 
+def add_kernel(a, b, out):
+    out[...] = (a[...].astype(F32) + b[...].astype(F32)).astype(BF)
+
+
 def rs2_kernel(*refs):
-    a, b, outs = refs[:4], refs[4:8], refs[8:]
+    a, b, outs = refs[:4], refs[4:9], refs[9:]
     swap = swap_matrix()
     for g in range((INT_A + INT_B) // 16):
         t = total4(a, 256 * g, 256) if g < 4 else total4(b, 256 * (g - 4), 256)
@@ -199,8 +203,8 @@
     for ref in small[:6]:
         ref[...] = t[60, at : at + ref.shape[0]]
         at += ref.shape[0]
-    for j in range(5):
-        small[6][j : j + 1, :] = t[60:61, at + 4 * j : at + 4 * j + 4]
+    for g in range(4):
+        small[6][g : g + 1, :] = t[60:61, at + 5 * g : at + 5 * g + 5]
     for cb in range(16):
         gate[:, cb * 128 : cb * 128 + 128] = t[64 + cb * 5 : 69 + cb * 5]
         up[:, cb * 128 : cb * 128 + 128] = t[144 + cb * 5 : 149 + cb * 5]
@@ -237,7 +241,7 @@
         wide[cb * 5 : cb * 5 + 5, :] = q[:, cb * 128 : cb * 128 + 128].astype(F32)
     for cb in range(4):
         wide[40 + cb * 5 : 45 + cb * 5, :] = kv[:, cb * 128 : cb * 128 + 128].astype(F32)
-    row = [ref[...].reshape(1, -1) for ref in (sq, skv, so, sg, su, sd)] + [gains[j : j + 1, :] for j in range(5)]
+    row = [ref[...].reshape(1, -1) for ref in (sq, skv, so, sg, su, sd)] + [gains[g : g + 1, :] for g in range(4)]
     v = jnp.concatenate(row + [jnp.zeros((1, 54), F32)], axis=1)
     hi = v.astype(BF).astype(F32)
     mid = (v - hi).astype(BF).astype(F32)
@@ -291,12 +295,19 @@
                 lkv[j * 128 + p * 16 : j * 128 + p * 16 + 16, cb * 128 : cb * 128 + 128] = level(ref[at : at + 16, :])
 
 
-def make_mask(segq, segk, mask):
+def column(row):
+    n = row.shape[1]
+    eye = lax.broadcasted_iota(jnp.int32, (n, n), 0) == lax.broadcasted_iota(jnp.int32, (n, n), 1)
+    return jnp.sum(jnp.where(eye, row.astype(F32), 0.0), axis=1, keepdims=True).astype(jnp.int32)
+
+
+def make_mask(segk, mask):
     for t in range(2):
+        mine = column(segk[:, WINDOW + t * 128 : WINDOW + t * 128 + 128])
         r = lax.broadcasted_iota(jnp.int32, (128, 640), 0)
         c = lax.broadcasted_iota(jnp.int32, (128, 640), 1)
         ok = (c <= WINDOW + r) & (c > r)
-        ok = ok & (segq[t * 128 : t * 128 + 128, :] == segk[:, t * 128 : t * 128 + 640])
+        ok = ok & (mine == segk[:, t * 128 : t * 128 + 640])
         mask[t] = ok.astype(F32)
 
 
@@ -315,15 +326,15 @@
 
 
 def first_kernel(
-    run, mine, theirs, dev_col, lane_of, dev_of, t0, t1, t2, dk, cos, sin, segq, segk,
-    par, h1p, q_out, kv_out, mix_out, lq, lkv, mask, sc, ex, tot,
+    run, mine, theirs, dev_row, lane_of, dev_of, t0, t1, t2, dk, cos, sin, segk,
+    par, h1p, q_out, kv_out, mix_out, lq, lkv, mask, sc, ex,
 ):
     lines = []
     for l in (60, 61, 62):
         refs = [piece(mine, theirs, p, RA) for p in range(8)]
         lines.append(jnp.concatenate([ref[at + l * 16 : at + l * 16 + 16, :] for ref, at in refs], axis=0))
     lines = jnp.concatenate(lines, axis=1)
-    devs = dev_col[...]
+    devs = column(dev_row[...])
     row = lax.broadcasted_iota(jnp.int32, (128, 256), 0)
     for i in range(NP // 256):
         cols = slice(i * 256, i * 256 + 256)
@@ -337,7 +348,7 @@
         v = t[...].astype(F32)
         h = v * lax.rsqrt(jnp.mean(v * v, axis=-1, keepdims=True) + EPS) * gain
         h1p[k * 256 : k * 256 + 256, :] = dot(h.astype(BF), perm).astype(BF)
-    make_mask(segq, segk, mask)
+    make_mask(segk, mask)
 
     def width(b, carry):
         @pl.when(run[b] == 0)
@@ -361,21 +372,17 @@
                 kv_out[b, k * 256 : k * 256 + 256, 0:256] = rope(key, cw, sw).astype(BF)
                 val = dot(rows, lkv[:, 256:]) * (par[:, OKV + 256 : OKV + 512] * U_D)
                 kv_out[b, k * 256 : k * 256 + 256, 256:512] = val.astype(BF)
+            ones = jnp.ones((640, 128), BF)
             for t in range(2):
-                keys = kv_out[b, t * 128 : t * 128 + 640, 0:256]
-                vals = kv_out[b, t * 128 : t * 128 + 640, 256:512]
-                sc[...] = dot_t(q_out[b, t], keys)
-
-                def soft(i, carry):
-                    at = pl.multiple_of(i * 32, 32)
-                    m = mask[t, pl.ds(pl.multiple_of((i % 4) * 32, 32), 32), :]
-                    e = jnp.exp2(jnp.tanh(sc[pl.ds(at, 32), :] * TANH_IN) * EXP2_IN) * m
-                    tot[pl.ds(at, 32), :] = jnp.broadcast_to(1.0 / jnp.sum(e, axis=1, keepdims=True), (32, 128))
-                    ex[pl.ds(at, 32), :] = e.astype(BF)
-                    return carry
-
-                lax.fori_loop(0, 16, soft, 0, unroll=4)
-                mixed = dot(ex[...], vals) * tot[:, 0:1]
+                sc[t] = dot_t(q_out[b, t], kv_out[b, t * 128 : t * 128 + 640, 0:256])
+            for t in range(2):
+                for i in range(16):
+                    rows = slice(i * 32, i * 32 + 32)
+                    m = mask[t, (i % 4) * 32 : (i % 4) * 32 + 32, :]
+                    ex[t, rows, :] = (jnp.exp2(jnp.tanh(sc[t, rows, :] * TANH_IN) * EXP2_IN) * m).astype(BF)
+                e = ex[t]
+                inv = 1.0 / dot(e, ones)
+                mixed = dot(e, kv_out[b, t * 128 : t * 128 + 640, 256:512]) * jnp.concatenate([inv, inv], axis=1)
                 for h in range(4):
                     mix_out[b, t * 128 : t * 128 + 128, h * 256 : h * 256 + 256] = mixed[h * 128 : h * 128 + 128].astype(BF)
 
@@ -395,7 +402,7 @@
 
 def middle_kernel(
     run, inat, mix, tok, cot, b0, b1, b2, b3, b4, b5, b6, b7, par, dk,
-    out, rest, gmix, g_mine, g_theirs, gpar,
+    out, rest, gmix, g0, g1_, g2_, g3_, g4, g5, g6, g7, gpar,
     pcs, lgu, ld, lo, onat, gu32, gate, up, aa, bb, hid, gg, gu, h2s, gbr, gat, att, mid, acc, perm, outv,
     in_sem, gu_sem, do_sem, out_sem,
 ):
@@ -422,9 +429,6 @@
             row = pl.multiple_of(inat[p * 16 + s] * 8, 8)
             for cb in range(5):
                 onat[pl.ds(row, 8), cb * 128 : cb * 128 + 128] = block[cb * 8 : cb * 8 + 8]
-    for copy in loads[1] + loads[2]:
-        copy.wait()
-
     def width(b, carry):
         rows = pl.ds(pl.multiple_of(b * TOK, TOK), TOK)
 
@@ -458,6 +462,11 @@
             h2 = (middle * r2 * g2).astype(BF)
             h2p = dot(h2, perm[...]).astype(BF)
             h2s[rows, :] = h2p
+
+            @pl.when(carry == 0)
+            def _():
+                for copy in loads[1] + loads[2]:
+                    copy.wait()
 
             def gate_up(f):
                 for half in range(2):
@@ -538,10 +547,7 @@
                 gpar[:, col_u] += sums[0:1, 256:512]
                 add = dot_t(both, lgu[:, f * 512 : f * 512 + 512])
                 acc[...] = add if f == 0 else acc[...] + add
-            g_h2 = acc[...]
-            high = g_h2.astype(BF)
-            low = (g_h2 - high.astype(F32)).astype(BF)
-            g_h2 = dot_t(high, perm[...]) + dot_t(low, perm[...])
+            g_h2 = dot_t(acc[...].astype(BF), perm[...])
             middle = mid[...]
             attended = att[...]
             gpar[:, ON + 2 * D : ON + 3 * D] += jnp.sum(g_h2 * middle * r2, axis=0, keepdims=True)
@@ -556,7 +562,7 @@
             gat[rows, :] = ga
             gmix[b] = dot_t(ga, lo[...]).astype(BF)
 
-        return carry
+        return carry + run[b]
 
     lax.fori_loop(0, 3, width, 0)
     out_copy = pltpu.make_async_copy(outv, out, out_sem)
@@ -570,8 +576,8 @@
     stores = []
 
     def leave(p, first, rows, sem):
-        to, base = piece(g_mine, g_theirs, p, RB)
-        copy = pltpu.make_async_copy(pcs.at[p, pl.ds(first, rows)], to.at[pl.ds(base + first, rows)], sem)
+        to = (g0, g1_, g2_, g3_, g4, g5, g6, g7)[p]
+        copy = pltpu.make_async_copy(pcs.at[p, pl.ds(first, rows)], to.at[pl.ds(first, rows)], sem)
         copy.start()
         stores.append(copy)
 
@@ -617,45 +623,82 @@
     out_copy.wait()
 
 
-def attn_back_kernel(
-    first, count, run, par, cos, sin, segq, segk, q, kv, gmix, gpar2,
-    gqb, gkvb, gpar,
-    mask, sc, gp, pb, gz, gq, gkv,
+def back_kernel(
+    run, par, cos, sin, segk, gpar_in, dk, dev_row, lane_of, dev_of,
+    q_far, kv_far, gmix_far, mine_far, theirs_far, h1p_far, t0_far, t1_far, t2_far,
+    own, back1, back2, g_mine, g_theirs,
+    q, kv, gmix, mine, theirs, h1p, toks, mask, sc, gp, ex, wt, pb, gz, gq, gkv, gq_sum, gkv_sum, gqb, gkvb, lq, lkv, gh1, gpar,
+    sem, sem_late,
 ):
-    make_mask(segq, segk, mask)
-    gpar[...] = gpar2[...]
-
-    def width(k, carry):
-        b = first + k
+    loads = [
+        [pltpu.make_async_copy(far.at[b], near.at[b], sem.at[b, k]) for k, (far, near) in enumerate(((q_far, q), (kv_far, kv), (gmix_far, gmix)))]
+        for b in range(3)
+    ]
+    late = [
+        pltpu.make_async_copy(far, near, sem_late.at[k])
+        for k, (far, near) in enumerate(((mine_far, mine), (theirs_far, theirs), (h1p_far, h1p)))
+    ]
+    last = [pltpu.make_async_copy(far, toks.at[k], sem_late.at[3 + k]) for k, far in enumerate((t0_far, t1_far, t2_far))]
+    for copy in loads[0] + late + loads[1] + loads[2] + last:
+        copy.start()
+    for t in range(2):
+        k = lax.broadcasted_iota(jnp.int32, (640, 128), 0)
+        r = lax.broadcasted_iota(jnp.int32, (640, 128), 1)
+        ok = (k <= WINDOW + r) & (k > r)
+        keys = jnp.concatenate([column(segk[:, (t + i) * 128 : (t + i + 1) * 128]) for i in range(5)], axis=0)
+        ok = ok & (keys == segk[:, WINDOW + t * 128 : WINDOW + t * 128 + 128])
+        mask[t] = ok.astype(F32)
+    gpar[...] = gpar_in[...]
+    gh1[...] = jnp.zeros_like(gh1)
+    gq_sum[...] = jnp.zeros_like(gq_sum)
+    gkv_sum[...] = jnp.zeros_like(gkv_sum)
+
+    def width(b, seen):
+        for k, (far, near) in enumerate(((q_far, q), (kv_far, kv), (gmix_far, gmix))):
+            pltpu.make_async_copy(far.at[b], near.at[b], sem.at[b, k]).wait()
+
         @pl.when(run[b] > 0)
         def _():
             gkv[...] = jnp.zeros_like(gkv)
+            gms = []
             for t in range(2):
-                win = slice(t * 128, t * 128 + 640)
-                keys = kv[b, win, 0:256]
-                vals = kv[b, win, 256:512]
                 gm = jnp.concatenate(
                     [gmix[b, t * 128 : t * 128 + 128, h * 256 : h * 256 + 256] for h in range(4)], axis=0
                 )
-                sc[...] = dot_t(q[b, t], keys)
-                gp[...] = dot_t(gm, vals)
-
-                def soft(i, carry):
-                    at = pl.multiple_of(i * 16, 16)
-                    m = mask[t, pl.ds(pl.multiple_of((i % 8) * 16, 16), 16), :]
-                    th = jnp.tanh(sc[pl.ds(at, 16), :] * TANH_IN)
-                    e = jnp.exp2(th * EXP2_IN) * m
-                    p = e * (1.0 / jnp.sum(e, axis=1, keepdims=True))
-                    pb[pl.ds(at, 16), :] = p.astype(BF)
-                    pg = p * gp[pl.ds(at, 16), :]
-                    dd = jnp.sum(pg, axis=1, keepdims=True)
-                    gz[pl.ds(at, 16), :] = ((pg - p * dd) * (1.0 - th * th)).astype(BF)
-                    return carry
-
-                lax.fori_loop(0, 32, soft, 0, unroll=4)
-                gkv[win, 256:512] += t_dot(pb[...], gm)
-                gkv[win, 0:256] += t_dot(gz[...], q[b, t]) * (1.0 / 16)
-                gq[t] = dot(gz[...], keys) * (1.0 / 16)
+                gms.append(gm)
+                sc[t] = dot_t(kv[b, t * 128 : t * 128 + 640, 0:256], q[b, t])
+                gp[t] = dot_t(kv[b, t * 128 : t * 128 + 640, 256:512], gm)
+            for t in range(2):
+                for h in range(4):
+                    cols = slice(h * 128, h * 128 + 128)
+                    total, dot_sum = jnp.zeros((16, 128), F32), jnp.zeros((16, 128), F32)
+                    for i in range(40):
+                        rows = slice(i * 16, i * 16 + 16)
+                        th = jnp.tanh(sc[t, rows, cols] * TANH_IN)
+                        e = jnp.exp2(th * EXP2_IN) * mask[t, rows, :]
+                        ex[t, rows, cols] = e
+                        wt[t, rows, cols] = 1.0 - th * th
+                        total = total + e
+                        dot_sum = dot_sum + e * gp[t, rows, cols]
+                    inv = 1.0 / jnp.sum(total, axis=0, keepdims=True)
+                    dd = jnp.sum(dot_sum, axis=0, keepdims=True) * inv
+                    inv, dd = jnp.broadcast_to(inv, (16, 128)), jnp.broadcast_to(dd, (16, 128))
+                    for i in range(40):
+                        rows = slice(i * 16, i * 16 + 16)
+                        p = ex[t, rows, cols] * inv
+                        pb[t, rows, cols] = p.astype(BF)
+                        gz[t, rows, cols] = (p * (gp[t, rows, cols] - dd) * wt[t, rows, cols]).astype(BF)
+                win = slice(t * 128, t * 128 + 640)
+                gkv[win, 256:512] += dot(pb[t], gms[t])
+                gkv[win, 0:256] += dot(gz[t], q[b, t]) * (1.0 / 16)
+                gq[t] = t_dot(gz[t], kv[b, win, 0:256]) * (1.0 / 16)
+
+            @pl.when(seen == 0)
+            def _():
+                for copy in late:
+                    copy.wait()
+
+            dequant_a(b, mine, theirs, lq, lkv)
             co, so = cos[512:768, :], sin[512:768, :]
             for h in range(4):
                 cols = slice(h * 256, h * 256 + 256)
@@ -664,7 +707,8 @@
                 raw = unrope(raw.astype(F32), co, so)
                 gpar[:, OQ + h * 256 : OQ + h * 256 + 256] += jnp.sum(g * raw, axis=0, keepdims=True)
                 g = g * (par[:, OQ + h * 256 : OQ + h * 256 + 256] * U_D)
-                gqb[k, :, cols] = g.astype(BF)
+                gq_sum[:, cols] += g
+                gqb[:, cols] = g.astype(BF)
             for w in range(3):
                 rows = slice(w * 256, w * 256 + 256)
                 cw, sw = cos[rows, :], sin[rows, :]
@@ -677,32 +721,16 @@
                     at = OKV + half * 256
                     gpar[:, at : at + 256] += jnp.sum(g * raw, axis=0, keepdims=True)
                     g = g * (par[:, at : at + 256] * U_D)
-                    gkvb[k, rows, cols] = g.astype(BF)
-
-        return carry
-
-    lax.fori_loop(0, count, width, 0)
-
-
-def last_kernel(
-    run, h1p, mine, theirs, gqb0, gkvb0, gqb1, gkvb1, par, gpar_in, dk, dev_col, lane_of, dev_of, t0, t1, t2,
-    own, back1, back2, g_mine, g_theirs,
-    lq, lkv, gh1, gpar, gq_sum, gkv_sum, gqs, gkvs,
-):
-    gh1[...] = jnp.zeros_like(gh1)
-    gpar[...] = gpar_in[...]
+                    gkv_sum[rows, cols] += g
+                    gkvb[rows, cols] = g.astype(BF)
+            gh1[512:768, :] += dot_t(gqb[...], lq[...])
+            for k in range(3):
+                gh1[k * 256 : k * 256 + 256, :] += dot_t(gkvb[k * 256 : k * 256 + 256, :], lkv[...])
+
+        return seen + run[b]
+
+    lax.fori_loop(0, 3, width, 0)
     gpar[:, OQ : OQ + 1536] = gpar[:, OQ : OQ + 1536] / par[:, OQ : OQ + 1536]
-    gq_sum[...] = jnp.zeros_like(gq_sum)
-    gkv_sum[...] = jnp.zeros_like(gkv_sum)
-    for b, (gqb, gkvb, at) in enumerate(((gqb0, gkvb0, 0), (gqb1, gkvb1, 0), (gqb1, gkvb1, 1))):
-
-        @pl.when(run[b] > 0)
-        def _(gqb=gqb, gkvb=gkvb, at=at):
-            gq_sum[...] += gqb[at].astype(F32)
-            gkv_sum[...] += gkvb[at].astype(F32)
-
-    gqs[...] = gq_sum[...].astype(BF)
-    gkvs[...] = gkv_sum[...].astype(BF)
 
     def put(w, first):
         for half in range(2):
@@ -713,34 +741,26 @@
                     k = j * 128 + p * 16
                     to[at : at + 16, :] = w[k : k + 16, half * 128 : half * 128 + 128]
 
+    gqb[...] = gq_sum[...].astype(BF)
+    gkvb[...] = gkv_sum[...].astype(BF)
     for f in range(4):
-        put(t_dot(h1p[512:768, :], gqs[:, f * 256 : f * 256 + 256]).astype(BF), f * 10)
+        put(t_dot(h1p[512:768, :], gqb[:, f * 256 : f * 256 + 256]).astype(BF), f * 10)
     for f in range(2):
-        put(t_dot(h1p[...], gkvs[:, f * 256 : f * 256 + 256]).astype(BF), 40 + f * 10)
-
-    for b, (gqb, gkvb, at) in enumerate(((gqb0, gkvb0, 0), (gqb1, gkvb1, 0), (gqb1, gkvb1, 1))):
-
-        @pl.when(run[b] > 0)
-        def _(b=b, gqb=gqb, gkvb=gkvb, at=at):
-            dequant_a(b, mine, theirs, lq, lkv)
-            gh1[512:768, :] += dot_t(gqb[at], lq[...])
-            for k in range(3):
-                gh1[k * 256 : k * 256 + 256, :] += dot_t(gkvb[at, k * 256 : k * 256 + 256, :], lkv[...])
-
+        put(t_dot(h1p[...], gkvb[:, f * 256 : f * 256 + 256]).astype(BF), 40 + f * 10)
+
+    for copy in last:
+        copy.wait()
     perm = perm_matrix(dk[...])
     gain_sum = jnp.zeros((1, D), F32)
-    for k, (t, to) in enumerate(((t0, back2), (t1, back1), (t2, own))):
-        g = gh1[k * 256 : k * 256 + 256, :]
-        high = g.astype(BF)
-        low = (g - high.astype(F32)).astype(BF)
-        g = dot_t(high, perm) + dot_t(low, perm)
-        v = t[...].astype(F32)
+    for k, to in enumerate((back2, back1, own)):
+        g = dot_t(gh1[k * 256 : k * 256 + 256, :].astype(BF), perm)
+        v = toks[k].astype(F32)
         r = lax.rsqrt(mean_of(v * v) + EPS)
         gain_sum = gain_sum + jnp.sum(g * v * r, axis=0, keepdims=True)
         to[...] = g.astype(to.dtype)
     gpar[:, ON : ON + D] = gain_sum
 
-    devs = dev_col[...]
+    devs = column(dev_row[...])
     sums = jnp.zeros((128, 128), F32)
     row = lax.broadcasted_iota(jnp.int32, (128, 256), 0)
     for i in range(NP // 256):
@@ -772,23 +792,23 @@
         args,
         scratch=[
             pltpu.VMEM((D, 1024), BF), pltpu.VMEM((D, 512), BF), pltpu.VMEM((2, 128, 640), F32),
-            pltpu.VMEM((512, 640), F32), pltpu.VMEM((512, 640), BF), pltpu.VMEM((512, 128), F32),
+            pltpu.VMEM((2, 512, 640), F32), pltpu.VMEM((2, 512, 640), BF),
         ],
-        in_specs=[SMEM] + [VMEM] * 13, name="first", us=20,
+        in_specs=[SMEM] + [VMEM] * 12, name="first", us=20,
     )
 
 
 def run_middle(args):
     out_shape = [
         sds((3, TOK, D), F32), sds((TOK, D), F32), sds((3, TOK, HEADS * HD), BF),
-        sds((4 * RB, 128), BF), sds((4 * RB, 128), BF), sds((1, NP), F32),
+        *[sds((RB, 128), BF)] * 8, sds((1, NP), F32),
     ]
     any_ = pl.BlockSpec(memory_space=pl.ANY)
     return pl.pallas_call(
         middle_kernel,
         out_shape=out_shape,
         in_specs=[SMEM, SMEM] + [VMEM] * 3 + [any_] * 8 + [VMEM] * 2,
-        out_specs=[any_, VMEM, VMEM, any_, any_, VMEM],
+        out_specs=[any_, VMEM, VMEM] + [any_] * 8 + [VMEM],
         scratch_shapes=[
             pltpu.VMEM((8, RB, 128), BF), pltpu.VMEM((D, 2 * FF), BF), pltpu.VMEM((FF, D), BF), pltpu.VMEM((1024, D), BF),
             pltpu.VMEM((1024, D), F32), pltpu.VMEM((2, TOK, 512), F32),
@@ -800,40 +820,32 @@
             pltpu.SemaphoreType.DMA((3, 8)), pltpu.SemaphoreType.DMA((4, 2, 8)), pltpu.SemaphoreType.DMA((2, 8)),
             pltpu.SemaphoreType.DMA,
         ],
-        compiler_params=pltpu.CompilerParams(vmem_limit_bytes=62 << 20),
+        compiler_params=pltpu.CompilerParams(vmem_limit_bytes=55 << 20),
         cost_estimate=cost_of(70),
         name="middle",
     )(*args)
 
 
-def run_attnb(first, count, args):
+def run_back(args):
     return call(
-        functools.partial(attn_back_kernel, first, count),
-        [sds((count, TOK, 1024), BF), sds((count, WIN, 512), BF), sds((1, NP), F32)],
-        args,
-        scratch=[
-            pltpu.VMEM((2, 128, 640), F32), pltpu.VMEM((512, 640), F32), pltpu.VMEM((512, 640), F32),
-            pltpu.VMEM((512, 640), BF), pltpu.VMEM((512, 640), BF),
-            pltpu.VMEM((2, 512, HD), F32), pltpu.VMEM((WIN, 512), F32),
-        ],
-        in_specs=[SMEM] + [VMEM] * 9, mem=28, name=f"attnb{first}", us=8 * count,
-    )
-
-
-def run_last(args):
-    return call(
-        last_kernel,
+        back_kernel,
         [
             sds((TOK, D), F32), sds((TOK, D), BF), sds((TOK, D), BF),
             sds((4 * RA, 128), BF), sds((4 * RA, 128), BF),
         ],
         args,
         scratch=[
-            pltpu.VMEM((D, 1024), BF), pltpu.VMEM((D, 512), BF),
-            pltpu.VMEM((WIN, D), F32), pltpu.VMEM((1, NP), F32),
+            pltpu.VMEM((3, 2, 512, HD), BF), pltpu.VMEM((3, WIN, 512), BF), pltpu.VMEM((3, TOK, 1024), BF),
+            pltpu.VMEM((4 * RA, 128), BF), pltpu.VMEM((4 * RA, 128), BF), pltpu.VMEM((WIN, D), BF), pltpu.VMEM((3, TOK, D), BF),
+            pltpu.VMEM((2, 640, 128), F32), pltpu.VMEM((2, 640, 512), F32), pltpu.VMEM((2, 640, 512), F32),
+            pltpu.VMEM((2, 640, 512), F32), pltpu.VMEM((2, 640, 512), F32),
+            pltpu.VMEM((2, 640, 512), BF), pltpu.VMEM((2, 640, 512), BF),
+            pltpu.VMEM((2, 512, HD), F32), pltpu.VMEM((WIN, 512), F32),
             pltpu.VMEM((TOK, 1024), F32), pltpu.VMEM((WIN, 512), F32), pltpu.VMEM((TOK, 1024), BF), pltpu.VMEM((WIN, 512), BF),
+            pltpu.VMEM((D, 1024), BF), pltpu.VMEM((D, 512), BF), pltpu.VMEM((WIN, D), F32), pltpu.VMEM((1, NP), F32),
+            pltpu.SemaphoreType.DMA((3, 3)), pltpu.SemaphoreType.DMA((6,)),
         ],
-        in_specs=[SMEM] + [VMEM] * 16, mem=28, name="last", us=14,
+        in_specs=[SMEM] + [VMEM] * 9 + [pl.BlockSpec(memory_space=pl.ANY)] * 9, mem=46, name="back", us=30,
     )
 
 
@@ -855,7 +867,7 @@
     )
     inat = ((((sz % 2) * 2 + core) * 2 + sz // 2) * 4 + sy) * 4 + sx
     dk = (5 * inat[None, :] + jnp.arange(5, dtype=jnp.int32)[:, None]).reshape(1, D)
-    dev_col = inat[:, None]
+    dev_row = inat[None, :]
 
     place = (y % 2) * 4 + x
     seq = zh * 2 + y // 2
@@ -863,7 +875,6 @@
     run = lax.dynamic_slice_in_dim(width_mask, seq, 1, 0)[0]
     padded = jnp.concatenate([jnp.full((1, WINDOW), -1, jnp.int32), segs], axis=1)
     segk = lax.dynamic_slice_in_dim(padded, place * TOK, WIN, 1)
-    segq = segk[0, WINDOW:][:, None]
     pos = (place * TOK - WINDOW + jnp.arange(WIN, dtype=jnp.int32)).astype(F32)
     inverse = 10000.0 ** (-2.0 * jnp.arange(HD // 2).astype(F32) / HD)
     angles = pos[:, None] * inverse[None, :]
@@ -871,44 +882,37 @@
 
     shard = call(
         pack_kernel, sds((N, 128), BF),
-        (q_codes, kv_codes, o_codes, gate_codes, up_codes, down_codes, q_scale, kv_scale, o_scale, gate_scale, up_scale, down_scale, norm_gains),
+        (q_codes, kv_codes, o_codes, gate_codes, up_codes, down_codes, q_scale, kv_scale, o_scale, gate_scale, up_scale, down_scale, norm_gains.T),
         scratch=[pltpu.VMEM((N, 128), F32)], name="pack", us=0,
     )
-    early = (run, inat, dk, dev_col, segq, segk, cos, sin)
+    early = (run, inat, dk, dev_row, segk, cos, sin)
     mine_a, theirs_a, mine_b, their_first, t0, t1, early = gather(shard, tokens, early)
-    run, inat, dk, dev_col, segq, segk, cos, sin = early
-
-    par, h1p, q, kv, mix = run_first((run, mine_a, theirs_a, dev_col, lane_of, dev_of, t0, t1, tokens, dk, cos, sin, segq, segk))
+    run, inat, dk, dev_row, segk, cos, sin = early
+
+    par, h1p, q, kv, mix = run_first((run, mine_a, theirs_a, dev_row, lane_of, dev_of, t0, t1, tokens, dk, cos, sin, segk))
     mix, *late = lax.optimization_barrier((mix, *mine_b[1:]))
     pieces_b = [mine_b[0], *late, their_first] + [other_core(b) for b in late]
-    out, rest, gmix, gm_b, gt_b, gpar = run_middle((run, inat, mix, tokens, cotangent, *pieces_b, par, dk))
-    got_b = other_core(gt_b)
-    gqb, gkvb = [], []
-    for first, count in ((0, 1), (1, 2)):
-        got = run_attnb(first, count, (run, par, cos, sin, segq, segk, q, kv, gmix, gpar))
-        gqb.append(got[0])
-        gkvb.append(got[1])
-        gpar = got[2]
-        if first == 0:
-            gpar, got_b = lax.optimization_barrier((gpar, got_b))
-            parts_b = first_hop(gm_b, got_b, RB, 2, 0)
-            gpar, parts_b[0] = lax.optimization_barrier((gpar, parts_b[0]))
-    own, back1, back2, gm_a, gt_a = run_last(
-        (run, h1p, mine_a, theirs_a, gqb[0], gkvb[0], gqb[1], gkvb[1], par, gpar, dk, dev_col, lane_of, dev_of, t0, t1, tokens)
+    out, rest, gmix, *g_b, gpar = run_middle((run, inat, mix, tokens, cotangent, *pieces_b, par, dk))
+    got_b = {r: other_core(g_b[4 + r]) for r in (2, 1, 3, 0)}
+    hop = {r: call(add_kernel, sds((RB, 128), BF), (g_b[r], got_b[r]), name=f"add{r}", mem=24, us=0) for r in (2, 1, 3)}
+    gpar, *hops = lax.optimization_barrier((gpar, hop[1], hop[2], hop[3]))
+    hops = [send(a, 2, -r) for r, a in zip((1, 2, 3), hops)]
+    own, back1, back2, gm_a, gt_a = run_back(
+        (run, par, cos, sin, segk, gpar, dk, dev_row, lane_of, dev_of, q, kv, gmix, mine_a, theirs_a, h1p, t0, t1, tokens)
     )
-    gt_a, *parts_b = lax.optimization_barrier((gt_a, *parts_b))
+    forth = lambda k: [(j, i) for i, j in behind(k)]
+    gt_a, *hops = lax.optimization_barrier((gt_a, *hops))
+    got1 = lax.ppermute(back1, ("y", "x"), forth(1))
+    got2 = lax.ppermute(back2, ("y", "x"), forth(2))
     parts_a = first_hop(gm_a, other_core(gt_a), RA, 1, 0)
     gq, gkv, gate, up, down, o, *small = scatter(
-        parts_a, parts_b,
+        parts_a, [g_b[0], got_b[0], *hops],
         [sds((5, 1024), F32), sds((5, 512), F32), sds((5, FF), F32), sds((5, FF), F32), sds((16, D), F32), sds((8, D), F32),
-         sds((8,), F32), sds((4,), F32), sds((5,), F32), sds((16,), F32), sds((16,), F32), sds((5,), F32), sds((5, 4), F32)],
+         sds((8,), F32), sds((4,), F32), sds((5,), F32), sds((16,), F32), sds((16,), F32), sds((5,), F32), sds((4, 5), F32)],
     )
-    forth = lambda k: [(j, i) for i, j in behind(k)]
-    got1 = lax.ppermute(back1, ("y", "x"), forth(1))
-    got2 = lax.ppermute(back2, ("y", "x"), forth(2))
     grad_tokens = call(end_kernel, sds((TOK, D), F32), (own, got1, got2, tokens, rest, par), name="end", mem=24, us=0)
 
-    return (out, grad_tokens, gq, gkv, o, gate, up, down, *small)
+    return (out, grad_tokens, gq, gkv, o, gate, up, down, *small[:6], small[6].T)
 
 
 def solution(mesh):

time: 245 us -> 229 us (0.935)
  the two profiles are of different devices: /device:TPU:8 before, /device:TPU:24 now
where the time goes in v2:
time: 229 us; the launch traced here: 225 us
  starting transfers between devices  80.1 us (35%)
  waiting for transfers between devices  68.5 us (30%)
  Pallas kernels  62.8 us (27%)
  local copies, waits for them, and re-layouts  7.77 us (3%)
  other arithmetic  4.52 us (2%)
    ppermute x24, starting transfers between devices, send(): return lax.ppermute(a, AX, stage_pairs(stage, r % 4))  54 us
    ppermute x24, waiting for transfers between devices, send(): return lax.ppermute(a, AX, stage_pairs(stage, r % 4))  53.4 us
    pallas_call x12, Pallas kernels, call(): pl.pallas_call(kernel, out_shape=out_shape, in_specs=in_specs or [VMEM] *...  33.8 us
    pallas_call x1, Pallas kernels, run_middle(): pl.pallas_call(middle_kernel, out_shape=out_shape, in_specs=[SMEM, SMEM]...  28.7 us
    ppermute x10, starting transfers between devices, other_core(): return lax.ppermute(a, 'c', [(0, 1), (1, 0)])  14.3 us
    ppermute x10, waiting for transfers between devices, other_core(): return lax.ppermute(a, 'c', [(0, 1), (1, 0)])  13.8 us
    ppermute x2, starting transfers between devices, gather(): t1, t0 = (lax.ppermute(tokens, ('y', 'x'), behind(k)) for k in (1, 2))  7.62 us
    unnamed x69, local copies, waits for them, and re-layouts  5.97 us
  transfers between devices with their start and end apart: 38, of which 26 were waited for; matrix products, arithmetic and copies ran while one was open for 3% of the time, Pallas kernels for 12%

profile of v2, /device:TPU:24, one launch (start us, length us, event | category | flops | bytes accessed | tf_op | source)
XLA Modules:
  0.0 225.3 jit_solution(14572799010854173777)
XLA Ops:
  2.3 2.8 %collective-permute-start.2 = (bf16[352,128]{1,0:T(8,128)(2,1)}, bf16[352,128]{1,0:T(8,128)(2,1)S(1)}, u32[]{:S(2)}, u32[]{:S(2)}) collective-permute-start(bf16[352,128]{1,0:T(8,128)(2,1)} %pack.1), channel_id=1, source_target_pairs={{0,3},{1,0},{2,1},{3,2},{4,7},{5,4},{6,5},{7,6},{8,11},{9,8},{10,9... | collective-permute-start | bytes 270344 | tf_op jit(solution)/shard_map/ppermute | solution.py:103
  6.7 3.7 %collective-permute-start.4 = (bf16[256,640]{1,0:T(8,128)(2,1)}, bf16[256,640]{1,0:T(8,128)(2,1)S(1)}, u32[]{:S(2)}, u32[]{:S(2)}) collective-permute-start(bf16[256,640]{1,0:T(8,128)(2,1)} %tok.3), channel_id=1, source_target_pairs={{0,1},{1,2},{2,3},{3,4},{4,5},{5,6},{6,7},{8,9},{9,10},{10,11},{11... | collective-permute-start | bytes 983048 | tf_op jit(solution)/shard_map/ppermute | solution.py:148
  10.5 3.9 %collective-permute-start.3 = (bf16[256,640]{1,0:T(8,128)(2,1)}, bf16[256,640]{1,0:T(8,128)(2,1)S(1)}, u32[]{:S(2)}, u32[]{:S(2)}) collective-permute-start(bf16[256,640]{1,0:T(8,128)(2,1)} %tok.3), channel_id=1, source_target_pairs={{0,2},{1,3},{2,4},{3,5},{4,6},{5,7},{8,10},{9,11},{10,12},{11,13},... | collective-permute-start | bytes 983048 | tf_op jit(solution)/shard_map/ppermute | solution.py:148
  18.9 2.2 collective-permute-start.5
  22.8 2.5 %multiply_sine_fusion = (f32[768,128]{1,0:T(8,128)}, f32[768,128]{1,0:T(8,128)}) fusion(f32[128]{0:T(128)S(1)} %multiply_power_fusion, f32[768]{0:T(1024)S(1)} %add_convert_fusion), kind=kLoop, calls=%fused_computation | loop fusion | flops 98304 | bytes 790016 | tf_op jit(solution)/shard_map/sin | solution.py:881
  26.6 3.1 %collective-permute-done.7.refs_3_ = bf16[1408,128]{1,0:T(8,128)(2,1)S(1)} collective-permute-done((bf16[1408,128]{1,0:T(8,128)(2,1)S(1)}, bf16[1408,128]{1,0:T(8,128)(2,1)S(1)}, u32[]{:S(2)}, u32[]{:S(2)}) %collective-permute-start.7) | collective-permute-done | bytes 360480 | tf_op jit(solution)/shard_map/ppermute | solution.py:103
  29.7 4.7 %collective-permute-done.5.refs_1_ = bf16[1408,128]{1,0:T(8,128)(2,1)} collective-permute-done((bf16[1408,128]{1,0:T(8,128)(2,1)S(1)}, bf16[1408,128]{1,0:T(8,128)(2,1)}, u32[]{:S(2)}, u32[]{:S(2)}) %collective-permute-start.5) | collective-permute-done | bytes 360480 | tf_op jit(solution)/shard_map/ppermute | solution.py:103
  34.4 3.0 %asm.1 = (bf16[1024,128]{1,0:T(8,128)(2,1)}, bf16[4608,128]{1,0:T(8,128)(2,1)}) custom-call(bf16[1408,128]{1,0:T(8,128)(2,1)} %copy-done.24, bf16[1408,128]{1,0:T(8,128)(2,1)} %collective-permute-done.5.refs_1_, bf16[1408,128]{1,0:T(8,128)(2,1)} %copy-done.29, bf16[1408,128]{1,0:T(8,128)(2,1)} %copy-done.28), custom_call_target="tpu_custom_call" | custom-call | flops 1000 | bytes 1000 | tf_op jit(solution)/shard_map/asm/pallas_call | solution.py:59
  37.4 4.0 %collective-permute-start.10 = (bf16[1024,128]{1,0:T(8,128)(2,1)}, bf16[1024,128]{1,0:T(8,128)(2,1)S(1)}, u32[]{:S(2)}, u32[]{:S(2)}) collective-permute-start(bf16[1024,128]{1,0:T(8,128)(2,1)} %get-tuple-element.89.a), channel_id=1, source_target_pairs={{0,80},{1,81},{2,82},{3,83},{4,84},{5,85},{6,86},{7,87},{8,88},{9,... | collective-permute-start | bytes 786440 | tf_op jit(solution)/shard_map/ppermute | solution.py:103
  44.7 2.3 %collective-permute-start.13 = (bf16[4608,128]{1,0:T(8,128)(2,1)}, bf16[4608,128]{1,0:T(8,128)(2,1)}, u32[]{:S(2)}, u32[]{:S(2)}) collective-permute-start(bf16[4608,128]{1,0:T(8,128)(2,1)} %get-tuple-element.98.b0), channel_id=1, source_target_pairs={{0,16},{1,17},{2,18},{3,19},{4,20},{5,21},{6,22},{7,23},{8,24},{9,... | collective-permute-start | bytes 3538952 | tf_op jit(solution)/shard_map/ppermute | solution.py:103
  49.6 2.4 %collective-permute-done.8.b = bf16[1024,128]{1,0:T(8,128)(2,1)S(1)} collective-permute-done((bf16[1024,128]{1,0:T(8,128)(2,1)}, bf16[1024,128]{1,0:T(8,128)(2,1)S(1)}, u32[]{:S(2)}, u32[]{:S(2)}) %collective-permute-start.8) | collective-permute-done | bytes 262176 | tf_op jit(solution)/shard_map/ppermute | solution.py:103
  52.8 2.2 join.1.mine.mine_far
  55.5 3.0 %collective-permute-done.11.theirs.theirs_far = bf16[4096,128]{1,0:T(8,128)(2,1)S(1)} collective-permute-done((bf16[4096,128]{1,0:T(8,128)(2,1)}, bf16[4096,128]{1,0:T(8,128)(2,1)S(1)}, u32[]{:S(2)}, u32[]{:S(2)}) %collective-permute-start.11) | collective-permute-done | bytes 1048608 | tf_op jit(solution)/shard_map/ppermute | solution.py:111
  59.5 10.8 %first.1 = (f32[1,9472]{1,0:T(1,128)}, bf16[768,640]{1,0:T(8,128)(2,1)}, bf16[3,2,512,256]{3,2,1,0:T(8,128)(2,1)}, bf16[3,768,512]{2,1,0:T(8,128)(2,1)}, bf16[3,256,1024]{2,1,0:T(8,128)(2,1)}) custom-call(s32[3]{0:T(128)} %fusion.4.run, bf16[4096,128]{1,0:T(8,128)(2,1)} %join.1.mine.mine_far, bf16[4096,128]{1,0:T(8,128)(2,1)} %copy-done.23, ...), custom_call_target="tpu_custom_call" | custom-call | flops 20001000 | bytes 1000 | tf_op jit(solution)/shard_map/first/pallas_call | solution.py:59
  70.2 3.5 %collective-permute-done.14.b3 = bf16[4608,128]{1,0:T(8,128)(2,1)} collective-permute-done((bf16[4608,128]{1,0:T(8,128)(2,1)}, bf16[4608,128]{1,0:T(8,128)(2,1)}, u32[]{:S(2)}, u32[]{:S(2)}) %collective-permute-start.14) | collective-permute-done | bytes 1179680 | tf_op jit(solution)/shard_map/ppermute | solution.py:103
  73.7 4.0 %collective-permute-done.12.b1 = bf16[4608,128]{1,0:T(8,128)(2,1)} collective-permute-done((bf16[4608,128]{1,0:T(8,128)(2,1)}, bf16[4608,128]{1,0:T(8,128)(2,1)}, u32[]{:S(2)}, u32[]{:S(2)}) %collective-permute-start.12) | collective-permute-done | bytes 1179680 | tf_op jit(solution)/shard_map/ppermute | solution.py:103
  78.8 2.5 %collective-permute-done.16.b5 = bf16[4608,128]{1,0:T(8,128)(2,1)S(1)} collective-permute-done((bf16[4608,128]{1,0:T(8,128)(2,1)}, bf16[4608,128]{1,0:T(8,128)(2,1)S(1)}, u32[]{:S(2)}, u32[]{:S(2)}) %collective-permute-start.16) | collective-permute-done | bytes 1179680 | tf_op jit(solution)/shard_map/ppermute | solution.py:111
  85.7 28.7 %middle.1 = (f32[3,256,640]{2,1,0:T(8,128)}, f32[256,640]{1,0:T(8,128)}, bf16[3,256,1024]{2,1,0:T(8,128)(2,1)}, bf16[4608,128]{1,0:T(8,128)(2,1)}, bf16[4608,128...) custom-call(s32[3]{0:T(128)} %fusion.4.run, ...), custom_call_target="tpu_custom_call" | custom-call | flops 70001000 | bytes 1000 | tf_op jit(solution)/shard_map/middle/pallas_call | solution.py:807
  114.4 11.8 %collective-permute-start.19 = (bf16[4608,128]{1,0:T(8,128)(2,1)}, bf16[4608,128]{1,0:T(8,128)(2,1)S(1)}, u32[]{:S(2)}, u32[]{:S(2)}) collective-permute-start(bf16[4608,128]{1,0:T(8,128)(2,1)} %get-tuple-element.107), channel_id=1, source_target_pairs={{0,32},{32,0},{1,33},{33,1},{2,34},{34,2},{3,35},{35,3},{4,36},{36... | collective-permute-start | bytes 3538952 | tf_op jit(solution)/shard_map/ppermute | solution.py:111
  126.7 2.2 collective-permute-done.19.b
  135.3 12.0 %back.1 = (f32[256,640]{1,0:T(8,128)S(1)}, bf16[256,640]{1,0:T(8,128)(2,1)S(1)}, bf16[256,640]{1,0:T(8,128)(2,1)S(1)}, bf16[4096,128]{1,0:T(8,128)(2,1)S(1)}, bf16[4096,128]{1,0:T(8,128)(2,1)S(1)}) custom-call(s32[3]{0:T(128)S(1)} %copy-done.21, f32[1,9472]{1,0:T(1,128)S(1)} %copy-done.15, f32[768,128]{1,0:T(8,128)S(1)} %copy-done.4, ...), custom_call_target="tpu_custom_call" | custom-call | flops 30001000 | bytes 1000 | tf_op jit(solution)/shard_map/back/pallas_call | solution.py:59
  149.4 2.5 %collective-permute-done.25.refs_7_ = bf16[4608,128]{1,0:T(8,128)(2,1)S(1)} collective-permute-done((bf16[4608,128]{1,0:T(8,128)(2,1)S(1)}, bf16[4608,128]{1,0:T(8,128)(2,1)S(1)}, u32[]{:S(2)}, u32[]{:S(2)}) %collective-permute-start.25) | collective-permute-done | bytes 1179680 | tf_op jit(solution)/shard_map/ppermute | solution.py:103
  151.8 12.5 %collective-permute-done.26.refs_8_ = bf16[4608,128]{1,0:T(8,128)(2,1)S(1)} collective-permute-done((bf16[4608,128]{1,0:T(8,128)(2,1)S(1)}, bf16[4608,128]{1,0:T(8,128)(2,1)S(1)}, u32[]{:S(2)}, u32[]{:S(2)}) %collective-permute-start.26) | collective-permute-done | bytes 1179680 | tf_op jit(solution)/shard_map/ppermute | solution.py:103
  169.6 4.1 %collective-permute-done.28.refs_1_ = bf16[1024,128]{1,0:T(8,128)(2,1)S(1)} collective-permute-done((bf16[1024,128]{1,0:T(8,128)(2,1)S(1)}, bf16[1024,128]{1,0:T(8,128)(2,1)S(1)}, u32[]{:S(2)}, u32[]{:S(2)}) %collective-permute-start.28) | collective-permute-done | bytes 262176 | tf_op jit(solution)/shard_map/ppermute | solution.py:103
  173.7 2.2 collective-permute-done.29.refs_2_
  175.9 2.7 %collective-permute-done.30.refs_3_ = bf16[1024,128]{1,0:T(8,128)(2,1)S(1)} collective-permute-done((bf16[1024,128]{1,0:T(8,128)(2,1)S(1)}, bf16[1024,128]{1,0:T(8,128)(2,1)S(1)}, u32[]{:S(2)}, u32[]{:S(2)}) %collective-permute-start.30) | collective-permute-done | bytes 262176 | tf_op jit(solution)/shard_map/ppermute | solution.py:103
  180.0 13.3 %collective-permute-start.33 = (bf16[1408,128]{1,0:T(8,128)(2,1)S(1)}, bf16[1408,128]{1,0:T(8,128)(2,1)S(1)}, u32[]{:S(2)}, u32[]{:S(2)}) collective-permute-start(bf16[1408,128]{1,0:T(8,128)(2,1)S(1)} %get-tuple-element.138), channel_id=1, source_target_pairs={{0,8},{1,9},{2,10},{3,11},{4,12},{5,13},{6,14},{7,15},{8,0},{9,1},... | collective-permute-start | bytes 1081352 | tf_op jit(solution)/shard_map/ppermute | solution.py:103
  193.3 2.5 %collective-permute-start.34 = (bf16[1408,128]{1,0:T(8,128)(2,1)S(1)}, bf16[1408,128]{1,0:T(8,128)(2,1)S(1)}, u32[]{:S(2)}, u32[]{:S(2)}) collective-permute-start(bf16[1408,128]{1,0:T(8,128)(2,1)S(1)} %get-tuple-element.139), channel_id=1, source_target_pairs={{0,4},{1,5},{2,6},{3,7},{4,8},{5,9},{6,10},{7,11},{8,12},{9,13},{1... | collective-permute-start | bytes 1081352 | tf_op jit(solution)/shard_map/ppermute | solution.py:103
  197.7 2.3 %collective-permute-start.23 = (bf16[256,640]{1,0:T(8,128)(2,1)S(1)}, bf16[256,640]{1,0:T(8,128)(2,1)S(1)}, u32[]{:S(2)}, u32[]{:S(2)}) collective-permute-start(bf16[256,640]{1,0:T(8,128)(2,1)S(1)} %get-tuple-element.119), channel_id=1, source_target_pairs={{2,0},{3,1},{4,2},{5,3},{6,4},{7,5},{10,8},{11,9},{12,10},{13,11},... | collective-permute-start | bytes 983048 | tf_op jit(solution)/shard_map/ppermute | solution.py:906
  200.0 2.4 %collective-permute-done.33.refs_2_ = bf16[1408,128]{1,0:T(8,128)(2,1)S(1)} collective-permute-done((bf16[1408,128]{1,0:T(8,128)(2,1)S(1)}, bf16[1408,128]{1,0:T(8,128)(2,1)S(1)}, u32[]{:S(2)}, u32[]{:S(2)}) %collective-permute-start.33) | collective-permute-done | bytes 360480 | tf_op jit(solution)/shard_map/ppermute | solution.py:103
  202.6 14.8 %collective-permute-start.35 = (bf16[352,128]{1,0:T(8,128)(2,1)S(1)}, bf16[352,128]{1,0:T(8,128)(2,1)S(1)}, u32[]{:S(2)}, u32[]{:S(2)}) collective-permute-start(bf16[352,128]{1,0:T(8,128)(2,1)S(1)} %get-tuple-element.141), channel_id=1, source_target_pairs={{0,3},{1,0},{2,1},{3,2},{4,7},{5,4},{6,5},{7,6},{8,11},{9,8},{10,9... | collective-permute-start | bytes 270344 | tf_op jit(solution)/shard_map/ppermute | solution.py:103
  220.4 3.1 %collective-permute-done.36.a2 = bf16[352,128]{1,0:T(8,128)(2,1)S(1)} collective-permute-done((bf16[352,128]{1,0:T(8,128)(2,1)S(1)}, bf16[352,128]{1,0:T(8,128)(2,1)S(1)}, u32[]{:S(2)}, u32[]{:S(2)}) %collective-permute-start.36) | collective-permute-done | bytes 90144 | tf_op jit(solution)/shard_map/ppermute | solution.py:103
  (137 shorter events, 46.0 us)
Async XLA Ops:
  2.3 13.8 %collective-permute-start.2 = (bf16[352,128]{1,0:T(8,128)(2,1)}, bf16[352,128]{1,0:T(8,128)(2,1)S(1)}, u32[]{:S(2)}, u32[]{:S(2)}) collective-permute-start(bf16[352,128]{1,0:T(8,128)(2,1)} %pack.1), channel_id=1, source_target_pairs={{0,3},{1,0},{2,1},{3,2},{4,7},{5,4},{6,5},{7,6},{8,11},{9,8},{10,9... | collective-permute-start | bytes 270344 | tf_op jit(solution)/shard_map/ppermute | solution.py:103
  5.1 11.1 %collective-permute-start.1 = (bf16[352,128]{1,0:T(8,128)(2,1)}, bf16[352,128]{1,0:T(8,128)(2,1)S(1)}, u32[]{:S(2)}, u32[]{:S(2)}) collective-permute-start(bf16[352,128]{1,0:T(8,128)(2,1)} %pack.1), channel_id=1, source_target_pairs={{0,2},{1,3},{2,0},{3,1},{4,6},{5,7},{6,4},{7,5},{8,10},{9,11},{10,... | collective-permute-start | bytes 270344 | tf_op jit(solution)/shard_map/ppermute | solution.py:103
  5.9 10.3 %collective-permute-start = (bf16[352,128]{1,0:T(8,128)(2,1)}, bf16[352,128]{1,0:T(8,128)(2,1)S(1)}, u32[]{:S(2)}, u32[]{:S(2)}) collective-permute-start(bf16[352,128]{1,0:T(8,128)(2,1)} %pack.1), channel_id=1, source_target_pairs={{0,1},{1,2},{2,3},{3,0},{4,5},{5,6},{6,7},{7,4},{8,9},{9,10},{10,1... | collective-permute-start | bytes 270344 | tf_op jit(solution)/shard_map/ppermute | solution.py:103
  6.7 18.6 %collective-permute-start.4 = (bf16[256,640]{1,0:T(8,128)(2,1)}, bf16[256,640]{1,0:T(8,128)(2,1)S(1)}, u32[]{:S(2)}, u32[]{:S(2)}) collective-permute-start(bf16[256,640]{1,0:T(8,128)(2,1)} %tok.3), channel_id=1, source_target_pairs={{0,1},{1,2},{2,3},{3,4},{4,5},{5,6},{6,7},{8,9},{9,10},{10,11},{11... | collective-permute-start | bytes 983048 | tf_op jit(solution)/shard_map/ppermute | solution.py:148
  10.5 16.1 %collective-permute-start.3 = (bf16[256,640]{1,0:T(8,128)(2,1)}, bf16[256,640]{1,0:T(8,128)(2,1)S(1)}, u32[]{:S(2)}, u32[]{:S(2)}) collective-permute-start(bf16[256,640]{1,0:T(8,128)(2,1)} %tok.3), channel_id=1, source_target_pairs={{0,2},{1,3},{2,4},{3,5},{4,6},{5,7},{8,10},{9,11},{10,12},{11,13},... | collective-permute-start | bytes 983048 | tf_op jit(solution)/shard_map/ppermute | solution.py:148
  17.1 12.6 %collective-permute-start.7 = (bf16[1408,128]{1,0:T(8,128)(2,1)S(1)}, bf16[1408,128]{1,0:T(8,128)(2,1)S(1)}, u32[]{:S(2)}, u32[]{:S(2)}) collective-permute-start(bf16[1408,128]{1,0:T(8,128)(2,1)S(1)} %pad_maximum_fusion.refs_0_), channel_id=1, source_target_pairs={{0,12},{1,13},{2,14},{3,15},{4,0},{5,1},{6,2},{7,3},{8,4},{9,5},{1... | collective-permute-start | bytes 1081352 | tf_op jit(solution)/shard_map/ppermute | solution.py:103
  17.9 11.7 %collective-permute-start.6 = (bf16[1408,128]{1,0:T(8,128)(2,1)S(1)}, bf16[1408,128]{1,0:T(8,128)(2,1)S(1)}, u32[]{:S(2)}, u32[]{:S(2)}) collective-permute-start(bf16[1408,128]{1,0:T(8,128)(2,1)S(1)} %pad_maximum_fusion.refs_0_), channel_id=1, source_target_pairs={{0,8},{1,9},{2,10},{3,11},{4,12},{5,13},{6,14},{7,15},{8,0},{9,1},... | collective-permute-start | bytes 1081352 | tf_op jit(solution)/shard_map/ppermute | solution.py:103
  18.9 15.5 %collective-permute-start.5 = (bf16[1408,128]{1,0:T(8,128)(2,1)S(1)}, bf16[1408,128]{1,0:T(8,128)(2,1)}, u32[]{:S(2)}, u32[]{:S(2)}) collective-permute-start(bf16[1408,128]{1,0:T(8,128)(2,1)S(1)} %pad_maximum_fusion.refs_0_), channel_id=1, source_target_pairs={{0,4},{1,5},{2,6},{3,7},{4,8},{5,9},{6,10},{7,11},{8,12},{9,13},{1... | collective-permute-start | bytes 1081352 | tf_op jit(solution)/shard_map/ppermute | solution.py:103
  37.4 11.1 %collective-permute-start.10 = (bf16[1024,128]{1,0:T(8,128)(2,1)}, bf16[1024,128]{1,0:T(8,128)(2,1)S(1)}, u32[]{:S(2)}, u32[]{:S(2)}) collective-permute-start(bf16[1024,128]{1,0:T(8,128)(2,1)} %get-tuple-element.89.a), channel_id=1, source_target_pairs={{0,80},{1,81},{2,82},{3,83},{4,84},{5,85},{6,86},{7,87},{8,88},{9,... | collective-permute-start | bytes 786440 | tf_op jit(solution)/shard_map/ppermute | solution.py:103
  41.4 8.2 %collective-permute-start.9 = (bf16[1024,128]{1,0:T(8,128)(2,1)}, bf16[1024,128]{1,0:T(8,128)(2,1)S(1)}, u32[]{:S(2)}, u32[]{:S(2)}) collective-permute-start(bf16[1024,128]{1,0:T(8,128)(2,1)} %get-tuple-element.89.a), channel_id=1, source_target_pairs={{0,16},{1,17},{2,18},{3,19},{4,20},{5,21},{6,22},{7,23},{8,24},{9,... | collective-permute-start | bytes 786440 | tf_op jit(solution)/shard_map/ppermute | solution.py:103
  41.5 10.6 %collective-permute-start.8 = (bf16[1024,128]{1,0:T(8,128)(2,1)}, bf16[1024,128]{1,0:T(8,128)(2,1)S(1)}, u32[]{:S(2)}, u32[]{:S(2)}) collective-permute-start(bf16[1024,128]{1,0:T(8,128)(2,1)} %get-tuple-element.89.a), channel_id=1, source_target_pairs={{0,64},{1,65},{2,66},{3,67},{4,68},{5,69},{6,70},{7,71},{8,72},{9,... | collective-permute-start | bytes 786440 | tf_op jit(solution)/shard_map/ppermute | solution.py:103
  42.7 31.0 %collective-permute-start.14 = (bf16[4608,128]{1,0:T(8,128)(2,1)}, bf16[4608,128]{1,0:T(8,128)(2,1)}, u32[]{:S(2)}, u32[]{:S(2)}) collective-permute-start(bf16[4608,128]{1,0:T(8,128)(2,1)} %get-tuple-element.98.b0), channel_id=1, source_target_pairs={{0,80},{1,81},{2,82},{3,83},{4,84},{5,85},{6,86},{7,87},{8,88},{9,... | collective-permute-start | bytes 3538952 | tf_op jit(solution)/shard_map/ppermute | solution.py:103
  44.7 29.1 %collective-permute-start.13 = (bf16[4608,128]{1,0:T(8,128)(2,1)}, bf16[4608,128]{1,0:T(8,128)(2,1)}, u32[]{:S(2)}, u32[]{:S(2)}) collective-permute-start(bf16[4608,128]{1,0:T(8,128)(2,1)} %get-tuple-element.98.b0), channel_id=1, source_target_pairs={{0,16},{1,17},{2,18},{3,19},{4,20},{5,21},{6,22},{7,23},{8,24},{9,... | collective-permute-start | bytes 3538952 | tf_op jit(solution)/shard_map/ppermute | solution.py:103
  48.5 29.3 %collective-permute-start.12 = (bf16[4608,128]{1,0:T(8,128)(2,1)}, bf16[4608,128]{1,0:T(8,128)(2,1)}, u32[]{:S(2)}, u32[]{:S(2)}) collective-permute-start(bf16[4608,128]{1,0:T(8,128)(2,1)} %get-tuple-element.98.b0), channel_id=1, source_target_pairs={{0,64},{1,65},{2,66},{3,67},{4,68},{5,69},{6,70},{7,71},{8,72},{9,... | collective-permute-start | bytes 3538952 | tf_op jit(solution)/shard_map/ppermute | solution.py:103
  55.0 23.8 %collective-permute-start.15 = (bf16[4608,128]{1,0:T(8,128)(2,1)}, bf16[4608,128]{1,0:T(8,128)(2,1)}, u32[]{:S(2)}, u32[]{:S(2)}) collective-permute-start(bf16[4608,128]{1,0:T(8,128)(2,1)} %get-tuple-element.98.b0), channel_id=1, source_target_pairs={{0,32},{32,0},{1,33},{33,1},{2,34},{34,2},{3,35},{35,3},{4,36},{36... | collective-permute-start | bytes 3538952 | tf_op jit(solution)/shard_map/ppermute | solution.py:111
  78.7 5.9 %collective-permute-start.18 = (bf16[4608,128]{1,0:T(8,128)(2,1)}, bf16[4608,128]{1,0:T(8,128)(2,1)S(1)}, u32[]{:S(2)}, u32[]{:S(2)}) collective-permute-start(bf16[4608,128]{1,0:T(8,128)(2,1)} %collective-permute-done.14.b3), channel_id=1, source_target_pairs={{0,32},{32,0},{1,33},{33,1},{2,34},{34,2},{3,35},{35,3},{4,36},{36... | collective-permute-start | bytes 3538952 | tf_op jit(solution)/shard_map/ppermute | solution.py:111
  114.4 14.4 %collective-permute-start.19 = (bf16[4608,128]{1,0:T(8,128)(2,1)}, bf16[4608,128]{1,0:T(8,128)(2,1)S(1)}, u32[]{:S(2)}, u32[]{:S(2)}) collective-permute-start(bf16[4608,128]{1,0:T(8,128)(2,1)} %get-tuple-element.107), channel_id=1, source_target_pairs={{0,32},{32,0},{1,33},{33,1},{2,34},{34,2},{3,35},{35,3},{4,36},{36... | collective-permute-start | bytes 3538952 | tf_op jit(solution)/shard_map/ppermute | solution.py:111
  126.3 6.0 %collective-permute-start.21 = (bf16[4608,128]{1,0:T(8,128)(2,1)}, bf16[4608,128]{1,0:T(8,128)(2,1)S(1)}, u32[]{:S(2)}, u32[]{:S(2)}) collective-permute-start(bf16[4608,128]{1,0:T(8,128)(2,1)} %get-tuple-element.111), channel_id=1, source_target_pairs={{0,32},{32,0},{1,33},{33,1},{2,34},{34,2},{3,35},{35,3},{4,36},{36... | collective-permute-start | bytes 3538952 | tf_op jit(solution)/shard_map/ppermute | solution.py:111
  133.1 16.3 %collective-permute-start.24 = (bf16[4608,128]{1,0:T(8,128)(2,1)S(1)}, bf16[4608,128]{1,0:T(8,128)(2,1)S(1)}, u32[]{:S(2)}, u32[]{:S(2)}) collective-permute-start(bf16[4608,128]{1,0:T(8,128)(2,1)S(1)} %add1.1), channel_id=1, source_target_pairs={{0,80},{1,81},{2,82},{3,83},{4,84},{5,85},{6,86},{7,87},{8,88},{9,... | collective-permute-start | bytes 3538952 | tf_op jit(solution)/shard_map/ppermute | solution.py:103
  134.0 17.8 %collective-permute-start.25 = (bf16[4608,128]{1,0:T(8,128)(2,1)S(1)}, bf16[4608,128]{1,0:T(8,128)(2,1)S(1)}, u32[]{:S(2)}, u32[]{:S(2)}) collective-permute-start(bf16[4608,128]{1,0:T(8,128)(2,1)S(1)} %add2.1), channel_id=1, source_target_pairs={{0,16},{1,17},{2,18},{3,19},{4,20},{5,21},{6,22},{7,23},{8,24},{9,... | collective-permute-start | bytes 3538952 | tf_op jit(solution)/shard_map/ppermute | solution.py:103
  134.0 30.3 %collective-permute-start.26 = (bf16[4608,128]{1,0:T(8,128)(2,1)S(1)}, bf16[4608,128]{1,0:T(8,128)(2,1)S(1)}, u32[]{:S(2)}, u32[]{:S(2)}) collective-permute-start(bf16[4608,128]{1,0:T(8,128)(2,1)S(1)} %add3.1), channel_id=1, source_target_pairs={{0,64},{1,65},{2,66},{3,67},{4,68},{5,69},{6,70},{7,71},{8,72},{9,... | collective-permute-start | bytes 3538952 | tf_op jit(solution)/shard_map/ppermute | solution.py:103
  167.3 6.4 %collective-permute-start.28 = (bf16[1024,128]{1,0:T(8,128)(2,1)S(1)}, bf16[1024,128]{1,0:T(8,128)(2,1)S(1)}, u32[]{:S(2)}, u32[]{:S(2)}) collective-permute-start(bf16[1024,128]{1,0:T(8,128)(2,1)S(1)} %get-tuple-element.128), channel_id=1, source_target_pairs={{0,80},{1,81},{2,82},{3,83},{4,84},{5,85},{6,86},{7,87},{8,88},{9,... | collective-permute-start | bytes 786440 | tf_op jit(solution)/shard_map/ppermute | solution.py:103
  168.0 8.0 %collective-permute-start.29 = (bf16[1024,128]{1,0:T(8,128)(2,1)S(1)}, bf16[1024,128]{1,0:T(8,128)(2,1)S(1)}, u32[]{:S(2)}, u32[]{:S(2)}) collective-permute-start(bf16[1024,128]{1,0:T(8,128)(2,1)S(1)} %get-tuple-element.129), channel_id=1, source_target_pairs={{0,16},{1,17},{2,18},{3,19},{4,20},{5,21},{6,22},{7,23},{8,24},{9,... | collective-permute-start | bytes 786440 | tf_op jit(solution)/shard_map/ppermute | solution.py:103
  168.0 10.7 %collective-permute-start.30 = (bf16[1024,128]{1,0:T(8,128)(2,1)S(1)}, bf16[1024,128]{1,0:T(8,128)(2,1)S(1)}, u32[]{:S(2)}, u32[]{:S(2)}) collective-permute-start(bf16[1024,128]{1,0:T(8,128)(2,1)S(1)} %get-tuple-element.130), channel_id=1, source_target_pairs={{0,64},{1,65},{2,66},{3,67},{4,68},{5,69},{6,70},{7,71},{8,72},{9,... | collective-permute-start | bytes 786440 | tf_op jit(solution)/shard_map/ppermute | solution.py:103
  179.9 20.1 %collective-permute-start.32 = (bf16[1408,128]{1,0:T(8,128)(2,1)S(1)}, bf16[1408,128]{1,0:T(8,128)(2,1)S(1)}, u32[]{:S(2)}, u32[]{:S(2)}) collective-permute-start(bf16[1408,128]{1,0:T(8,128)(2,1)S(1)} %get-tuple-element.137), channel_id=1, source_target_pairs={{0,12},{1,13},{2,14},{3,15},{4,0},{5,1},{6,2},{7,3},{8,4},{9,5},{1... | collective-permute-start | bytes 1081352 | tf_op jit(solution)/shard_map/ppermute | solution.py:103
  180.0 22.5 %collective-permute-start.33 = (bf16[1408,128]{1,0:T(8,128)(2,1)S(1)}, bf16[1408,128]{1,0:T(8,128)(2,1)S(1)}, u32[]{:S(2)}, u32[]{:S(2)}) collective-permute-start(bf16[1408,128]{1,0:T(8,128)(2,1)S(1)} %get-tuple-element.138), channel_id=1, source_target_pairs={{0,8},{1,9},{2,10},{3,11},{4,12},{5,13},{6,14},{7,15},{8,0},{9,1},... | collective-permute-start | bytes 1081352 | tf_op jit(solution)/shard_map/ppermute | solution.py:103
  193.3 9.2 %collective-permute-start.34 = (bf16[1408,128]{1,0:T(8,128)(2,1)S(1)}, bf16[1408,128]{1,0:T(8,128)(2,1)S(1)}, u32[]{:S(2)}, u32[]{:S(2)}) collective-permute-start(bf16[1408,128]{1,0:T(8,128)(2,1)S(1)} %get-tuple-element.139), channel_id=1, source_target_pairs={{0,4},{1,5},{2,6},{3,7},{4,8},{5,9},{6,10},{7,11},{8,12},{9,13},{1... | collective-permute-start | bytes 1081352 | tf_op jit(solution)/shard_map/ppermute | solution.py:103
  195.8 22.5 %collective-permute-start.22 = (bf16[256,640]{1,0:T(8,128)(2,1)S(1)}, bf16[256,640]{1,0:T(8,128)(2,1)S(1)}, u32[]{:S(2)}, u32[]{:S(2)}) collective-permute-start(bf16[256,640]{1,0:T(8,128)(2,1)S(1)} %get-tuple-element.118), channel_id=1, source_target_pairs={{1,0},{2,1},{3,2},{4,3},{5,4},{6,5},{7,6},{9,8},{10,9},{11,10},{12... | collective-permute-start | bytes 983048 | tf_op jit(solution)/shard_map/ppermute | solution.py:905
  197.7 20.6 %collective-permute-start.23 = (bf16[256,640]{1,0:T(8,128)(2,1)S(1)}, bf16[256,640]{1,0:T(8,128)(2,1)S(1)}, u32[]{:S(2)}, u32[]{:S(2)}) collective-permute-start(bf16[256,640]{1,0:T(8,128)(2,1)S(1)} %get-tuple-element.119), channel_id=1, source_target_pairs={{2,0},{3,1},{4,2},{5,3},{6,4},{7,5},{10,8},{11,9},{12,10},{13,11},... | collective-permute-start | bytes 983048 | tf_op jit(solution)/shard_map/ppermute | solution.py:906
  202.6 17.8 %collective-permute-start.35 = (bf16[352,128]{1,0:T(8,128)(2,1)S(1)}, bf16[352,128]{1,0:T(8,128)(2,1)S(1)}, u32[]{:S(2)}, u32[]{:S(2)}) collective-permute-start(bf16[352,128]{1,0:T(8,128)(2,1)S(1)} %get-tuple-element.141), channel_id=1, source_target_pairs={{0,3},{1,0},{2,1},{3,2},{4,7},{5,4},{6,5},{7,6},{8,11},{9,8},{10,9... | collective-permute-start | bytes 270344 | tf_op jit(solution)/shard_map/ppermute | solution.py:103
  217.4 6.1 %collective-permute-start.36 = (bf16[352,128]{1,0:T(8,128)(2,1)S(1)}, bf16[352,128]{1,0:T(8,128)(2,1)S(1)}, u32[]{:S(2)}, u32[]{:S(2)}) collective-permute-start(bf16[352,128]{1,0:T(8,128)(2,1)S(1)} %get-tuple-element.142), channel_id=1, source_target_pairs={{0,2},{1,3},{2,0},{3,1},{4,6},{5,7},{6,4},{7,5},{8,10},{9,11},{10,... | collective-permute-start | bytes 270344 | tf_op jit(solution)/shard_map/ppermute | solution.py:103
  217.4 6.7 %collective-permute-start.37 = (bf16[352,128]{1,0:T(8,128)(2,1)S(1)}, bf16[352,128]{1,0:T(8,128)(2,1)S(1)}, u32[]{:S(2)}, u32[]{:S(2)}) collective-permute-start(bf16[352,128]{1,0:T(8,128)(2,1)S(1)} %get-tuple-element.143), channel_id=1, source_target_pairs={{0,1},{1,2},{2,3},{3,0},{4,5},{5,6},{6,7},{7,4},{8,9},{9,10},{10,1... | collective-permute-start | bytes 270344 | tf_op jit(solution)/shard_map/ppermute | solution.py:103
  (40 other events, 278.6 us)
